TPU v7x, 32 devices: a whole 2x2x4 slice. The times are simulated.
32 devices in a mesh: gx: 16 (over z, y, core), gy: 2 (over x).
Axes of the slice: x: 2, y: 2, z: 4, core: 2. Of those that a mesh axis runs over, the one named last changes fastest.
Arguments:
- pops: float32 [19, 64, 16, 128], P(None, 'gx', 'gy'), may hold values from 0.005 to 0.5, as said below
- label: int32 [64, 16, 128], P('gx', 'gy'), may hold values from 0 to 2, as said below
- drive: float32 [3, 64, 16, 128], P(None, 'gx', 'gy'), may hold values from -0.3 to 0.3
Outputs:
- momentum: float32 [3, 64, 16, 128], P(None, 'gx', 'gy')
- running: float32 [3, 16, 4, 32], P(None, 'gx', 'gy')
Inputs may be any that keep to these rules, and one draw needn't show every extreme that they name: `pops`: populations near a local equilibrium with density 0.8 to 1.2 and each velocity component within 0.1. `label`: 2 marks walls: every cell with z index 0 or 127, and scattered obstacle cells; elsewhere 1 marks the second solution, 0 the first.
All inputs are finite; a program needn't handle non-finite values.
Results may differ from a plain program's by a relative error of at most 0.0003.
Values sent between devices are 32-bit elements; how exact they have to be, the bound alone decides.
A program may use at most 64 MiB of HBM per device.

v0:
```python
import math

import jax
import jax.numpy as jnp
from jax import lax
from jax.sharding import PartitionSpec as P

NZ = 128
STEPS = 4


VELOCITY = [
    [0, 0, 0],
    [1, 0, 0],
    [-1, 0, 0],
    [0, 1, 0],
    [0, -1, 0],
    [0, 0, 1],
    [0, 0, -1],
    [1, 1, 0],
    [-1, -1, 0],
    [1, -1, 0],
    [-1, 1, 0],
    [1, 0, 1],
    [-1, 0, -1],
    [1, 0, -1],
    [-1, 0, 1],
    [0, 1, 1],
    [0, -1, -1],
    [0, 1, -1],
    [0, -1, 1],
]
OPPOSITE = [0, 2, 1, 4, 3, 6, 5, 8, 7, 10, 9, 12, 11, 14, 13, 16, 15, 18, 17]
WEIGHTS = [1.0 / 3.0] + [1.0 / 18.0] * 6 + [1.0 / 36.0] * 12
PAIRS = [(0, 0), (1, 1), (2, 2), (0, 1), (0, 2), (1, 2)]
COMPONENT = [[0, 3, 4], [3, 1, 5], [4, 5, 2]]
SLOW_VISCOSITY = 0.0004


def with_halo(cells, sides, width):
    for axis, dim in sides:
        count = lax.axis_size(axis)
        head = lax.slice_in_dim(cells, 0, width, axis=dim)
        tail = lax.slice_in_dim(cells, cells.shape[dim] - width, cells.shape[dim], axis=dim)
        cells = jnp.concatenate(
            [
                lax.ppermute(tail, axis, [(i, (i + 1) % count) for i in range(count)]),
                cells,
                lax.ppermute(head, axis, [((i + 1) % count, i) for i in range(count)]),
            ],
            axis=dim,
        )
    return cells


def collide(pops, label, drive, phase):
    columns = [
        jnp.array([row[axis_id] for row in VELOCITY], jnp.float32).reshape(19, 1, 1, 1)
        for axis_id in range(3)
    ]
    weights = jnp.array(WEIGHTS, jnp.float32).reshape(19, 1, 1, 1)
    density = jnp.sum(pops, axis=0)
    moment = [jnp.sum(columns[axis_id] * pops, axis=0) for axis_id in range(3)]
    speed = [moment[axis_id] / density for axis_id in range(3)]
    along = columns[0] * speed[0] + columns[1] * speed[1] + columns[2] * speed[2]
    square = speed[0] * speed[0] + speed[1] * speed[1] + speed[2] * speed[2]
    balance = weights * density * (1.0 + 3.0 * along + 4.5 * along * along - 1.5 * square)
    second = label == 1
    solid = label == 2
    omega = jnp.where(second, 1.1, 1.6)
    strength = jnp.where(second, 0.6, 1.0) * phase
    push = columns[0] * drive[0] + columns[1] * drive[1] + columns[2] * drive[2]
    relaxed = pops - omega * (pops - balance) + 3.0 * weights * strength * push
    bounced = jnp.stack([pops[other] for other in OPPOSITE])
    post = jnp.where(solid, bounced, relaxed)
    fluid = jnp.where(solid, 0.0, 1.0)
    stress = jnp.stack([moment[first] * moment[later] / density * fluid for first, later in PAIRS])
    return (post, stress)


def momentum_of(pops):
    columns = [
        jnp.array([row[axis_id] for row in VELOCITY], jnp.float32).reshape(19, 1, 1, 1)
        for axis_id in range(3)
    ]
    return jnp.stack([jnp.sum(columns[axis_id] * pops, axis=0) for axis_id in range(3)])


def tables(length):
    index = jnp.arange(length, dtype=jnp.int32)
    turns = index[:, None] * index[None, :] % length
    angle = turns.astype(jnp.float32) * (2.0 * math.pi / length)
    return (jnp.cos(angle), jnp.sin(angle))


def product(values, table):
    return jnp.matmul(values, table, precision=lax.Precision.HIGHEST)


def transform(real, imag, axis_id, inverse):
    length = real.shape[axis_id]
    cosine, sine = tables(length)
    real_last = jnp.moveaxis(real, axis_id, -1)
    imag_last = jnp.moveaxis(imag, axis_id, -1)
    if inverse:
        out_real = (product(real_last, cosine) - product(imag_last, sine)) / length
        out_imag = (product(imag_last, cosine) + product(real_last, sine)) / length
    else:
        out_real = product(real_last, cosine) + product(imag_last, sine)
        out_imag = product(imag_last, cosine) - product(real_last, sine)
    return (jnp.moveaxis(out_real, -1, axis_id), jnp.moveaxis(out_imag, -1, axis_id))


def wavenumber(index, length):
    shifted = index - length * (index >= (length + 1) // 2).astype(jnp.int32)
    return shifted.astype(jnp.float32) * (2.0 * math.pi / length)


def local(pops, label, drive):
    width = pops.shape[1]
    height = pops.shape[2]
    state = pops
    total = jnp.zeros((6,) + pops.shape[1:], jnp.float32)
    for step in range(STEPS):
        phase = math.cos(2.0 * math.pi * (step + 0.5) / STEPS)
        post, stress = collide(state, label, drive, phase)
        total = total + stress
        padded = with_halo(post, (("gx", 1), ("gy", 2)), 1)
        moved = []
        for index in range(19):
            start_x = 1 - VELOCITY[index][0]
            start_y = 1 - VELOCITY[index][1]
            piece = padded[index, start_x : start_x + width, start_y : start_y + height, :]
            moved.append(jnp.roll(piece, VELOCITY[index][2], axis=2))
        state = jnp.stack(moved)
    momentum = momentum_of(state)
    block_x = width // 4
    block_y = height // 4
    slow_z = NZ // 4
    slow = (total / STEPS).reshape(6, block_x, 4, block_y, 4, slow_z, 4).mean(axis=(2, 4, 6))
    cosine_z, sine_z = tables(slow_z)
    spectrum = jnp.stack([product(slow, cosine_z), -product(slow, sine_z)])
    spectrum = lax.all_to_all(spectrum, "gy", split_axis=4, concat_axis=3, tiled=True)
    full_y = spectrum.shape[3]
    part_z = spectrum.shape[4]
    real, imag = transform(spectrum[0], spectrum[1], 2, False)
    spectrum = jnp.stack([real, imag]).reshape(2, 6, block_x, full_y * part_z)
    spectrum = lax.all_to_all(spectrum, "gx", split_axis=3, concat_axis=2, tiled=True)
    full_x = spectrum.shape[2]
    part_m = spectrum.shape[3]
    real, imag = transform(spectrum[0], spectrum[1], 1, False)
    wave_x = wavenumber(jnp.arange(full_x, dtype=jnp.int32), full_x).reshape(full_x, 1)
    flat = lax.axis_index("gx") * part_m + jnp.arange(part_m, dtype=jnp.int32)
    row_y = flat // part_z
    index_z = lax.axis_index("gy") * part_z + flat % part_z
    wave_y = wavenumber(row_y, full_y).reshape(1, part_m)
    wave_z = wavenumber(index_z, slow_z).reshape(1, part_m)
    waves = [wave_x, wave_y, wave_z]
    force_real = [
        waves[0] * imag[COMPONENT[first][0]]
        + waves[1] * imag[COMPONENT[first][1]]
        + waves[2] * imag[COMPONENT[first][2]]
        for first in range(3)
    ]
    force_imag = [
        -(
            waves[0] * real[COMPONENT[first][0]]
            + waves[1] * real[COMPONENT[first][1]]
            + waves[2] * real[COMPONENT[first][2]]
        )
        for first in range(3)
    ]
    wave_sq = wave_x * wave_x + wave_y * wave_y + wave_z * wave_z
    positive = wave_sq > 0
    safe = jnp.where(positive, wave_sq, 1.0)
    inner_real = waves[0] * force_real[0] + waves[1] * force_real[1] + waves[2] * force_real[2]
    inner_imag = waves[0] * force_imag[0] + waves[1] * force_imag[1] + waves[2] * force_imag[2]
    speed_real = jnp.stack(
        [
            jnp.where(
                positive,
                (force_real[first] - waves[first] * inner_real / safe) / (SLOW_VISCOSITY * safe),
                0.0,
            )
            for first in range(3)
        ]
    )
    speed_imag = jnp.stack(
        [
            jnp.where(
                positive,
                (force_imag[first] - waves[first] * inner_imag / safe) / (SLOW_VISCOSITY * safe),
                0.0,
            )
            for first in range(3)
        ]
    )
    real, imag = transform(speed_real, speed_imag, 1, True)
    result = lax.all_to_all(jnp.stack([real, imag]), "gx", split_axis=2, concat_axis=3, tiled=True)
    result = result.reshape(2, 3, block_x, full_y, part_z)
    real, imag = transform(result[0], result[1], 2, True)
    result = lax.all_to_all(jnp.stack([real, imag]), "gy", split_axis=3, concat_axis=4, tiled=True)
    running = (product(result[0], cosine_z) - product(result[1], sine_z)) / slow_z
    return (momentum, running)


def solution(mesh):
    in_specs = (P(None, "gx", "gy", None), P("gx", "gy", None), P(None, "gx", "gy", None))
    out_specs = (P(None, "gx", "gy", None), P(None, "gx", "gy", None))
    return jax.shard_map(local, mesh=mesh, in_specs=in_specs, out_specs=out_specs, check_vma=False)
```

profile of v0, /device:TPU:0, one launch (start us, length us, event | category | flops | bytes accessed | tf_op | source)
XLA Modules:
  0.0 148.5 jit_solution(7120964954099912545)
XLA Ops:
  11.3 5.5 %collective-permute-start = (f32[19,1,8,128]{3,2,1,0:T(8,128)S(1)}, f32[19,1,8,128]{3,2,1,0:T(8,128)S(1)}, u32[]{:S(2)}, u32[]{:S(2)}) collective-permute-start(f32[19,1,8,128]{3,2,1,0:T(8,128)S(1)} %get-tuple-element.234), channel_id=1, source_target_pairs={{2,0},{4,2},{6,4},{8,6},{10,8},{12,10},{14,12},{16,14},{18,16},{20... | collective-permute-start | bytes 233480 | tf_op jit(solution)/shard_map/ppermute | solution.py:49
  23.6 1.6 %collective-permute-start.3 = (f32[19,6,1,128]{3,2,1,0:T(1,128)S(1)}, f32[19,6,1,128]{3,2,1,0:T(1,128)S(1)}, u32[]{:S(2)}, u32[]{:S(2)}) collective-permute-start(f32[19,6,1,128]{3,2,1,0:T(1,128)S(1)} %get-tuple-element.202), channel_id=1, source_target_pairs={{0,1},{1,0},{2,3},{3,2},{4,5},{5,4},{6,7},{7,6},{8,9},{9,8},{10,11... | collective-permute-start | bytes 175112 | tf_op jit(solution)/shard_map/ppermute | solution.py:47
  25.7 2.1 %collective-permute-done.3 = f32[19,6,1,128]{3,2,1,0:T(1,128)S(1)} collective-permute-done((f32[19,6,1,128]{3,2,1,0:T(1,128)S(1)}, f32[19,6,1,128]{3,2,1,0:T(1,128)S(1)}, u32[]{:S(2)}, u32[]{:S(2)}) %collective-permute-start.3) | collective-permute-done | bytes 58400 | tf_op jit(solution)/shard_map/ppermute | solution.py:47
  28.0 1.3 collective-permute-done.2
  31.6 3.1 %collective-permute-start.4 = (f32[19,1,8,128]{3,2,1,0:T(8,128)S(1)}, f32[19,1,8,128]{3,2,1,0:T(8,128)S(1)}, u32[]{:S(2)}, u32[]{:S(2)}) collective-permute-start(f32[19,1,8,128]{3,2,1,0:T(8,128)S(1)} %get-tuple-element.230), channel_id=1, source_target_pairs={{2,0},{4,2},{6,4},{8,6},{10,8},{12,10},{14,12},{16,14},{18,16},{20... | collective-permute-start | bytes 233480 | tf_op jit(solution)/shard_map/ppermute | solution.py:49
  35.5 1.2 collective-permute-done.4
  36.7 4.5 %collective-permute-done.5 = f32[19,1,8,128]{3,2,1,0:T(8,128)S(1)} collective-permute-done((f32[19,1,8,128]{3,2,1,0:T(8,128)S(1)}, f32[19,1,8,128]{3,2,1,0:T(8,128)S(1)}, u32[]{:S(2)}, u32[]{:S(2)}) %collective-permute-start.5) | collective-permute-done | bytes 77856 | tf_op jit(solution)/shard_map/ppermute | solution.py:47
  41.3 1.0 collective-permute-start.7
  42.2 1.1 collective-permute-start.6
  43.4 2.1 %collective-permute-done.7 = f32[19,6,1,128]{3,2,1,0:T(1,128)S(1)} collective-permute-done((f32[19,6,1,128]{3,2,1,0:T(1,128)S(1)}, f32[19,6,1,128]{3,2,1,0:T(1,128)S(1)}, u32[]{:S(2)}, u32[]{:S(2)}) %collective-permute-start.7) | collective-permute-done | bytes 58400 | tf_op jit(solution)/shard_map/ppermute | solution.py:47
  50.8 4.7 %collective-permute-done.9 = f32[19,1,8,128]{3,2,1,0:T(8,128)S(1)} collective-permute-done((f32[19,1,8,128]{3,2,1,0:T(8,128)S(1)}, f32[19,1,8,128]{3,2,1,0:T(8,128)S(1)}, u32[]{:S(2)}, u32[]{:S(2)}) %collective-permute-start.9) | collective-permute-done | bytes 77856 | tf_op jit(solution)/shard_map/ppermute | solution.py:47
  55.6 1.2 collective-permute-start.11
  56.8 0.9 collective-permute-start.10
  57.7 2.1 %collective-permute-done.11 = f32[19,6,1,128]{3,2,1,0:T(1,128)S(1)} collective-permute-done((f32[19,6,1,128]{3,2,1,0:T(1,128)S(1)}, f32[19,6,1,128]{3,2,1,0:T(1,128)S(1)}, u32[]{:S(2)}, u32[]{:S(2)}) %collective-permute-start.11) | collective-permute-done | bytes 58400 | tf_op jit(solution)/shard_map/ppermute | solution.py:47
  60.0 1.0 collective-permute-done.10
  73.6 0.9 copy.108
  76.7 1.2 stack.384
  78.8 1.2 stack.385
  81.0 1.2 stack.386
  83.1 1.2 stack.387
  93.6 3.2 %all-to-all-start = ((f32[2,1,384]{2,1,0:T(1,128)}), f32[2,1,384]{2,1,0:T(1,128)S(1)}, u32[]{:S(2)}, u32[]{:S(2)}) async-start(f32[2,1,384]{2,1,0:T(1,128)} %reshape.1616), calls=%async_computation | async-start | bytes 6144 | tf_op jit(solution)/shard_map/all_to_all | solution.py:143
  96.9 3.8 %all-to-all-done = f32[2,1,384]{2,1,0:T(1,128)S(1)} async-done(((f32[2,1,384]{2,1,0:T(1,128)}), f32[2,1,384]{2,1,0:T(1,128)S(1)}, u32[]{:S(2)}, u32[]{:S(2)}) %all-to-all-start) | async-done | bytes 3104 | tf_op jit(solution)/shard_map/all_to_all | solution.py:143
  103.8 3.8 %all-to-all-start.1 = ((f32[2,6,1,64]{1,0,2,3:T(2,128)}), f32[2,6,1,64]{1,0,2,3:T(2,128)S(1)}, u32[]{:S(2)}, u32[]{:S(2)}) async-start(f32[2,6,1,64]{1,0,2,3:T(2,128)} %copy.123), calls=%async_computation.1 | async-start | bytes 131072 | tf_op jit(solution)/shard_map/all_to_all | solution.py:148
  108.8 5.6 %all-to-all-done.1 = f32[2,6,1,64]{1,0,2,3:T(2,128)S(1)} async-done(((f32[2,6,1,64]{1,0,2,3:T(2,128)}), f32[2,6,1,64]{1,0,2,3:T(2,128)S(1)}, u32[]{:S(2)}, u32[]{:S(2)}) %all-to-all-start.1) | async-done | bytes 3104 | tf_op jit(solution)/shard_map/all_to_all | solution.py:148
  118.1 3.5 %all-to-all-start.2 = ((f32[2,3,16,4]{3,0,1,2:T(2,128)}), f32[2,3,16,4]{3,0,1,2:T(2,128)S(1)}, u32[]{:S(2)}, u32[]{:S(2)}) async-start(f32[2,3,16,4]{3,0,1,2:T(2,128)} %copy.128), calls=%async_computation.2 | async-start | bytes 98304 | tf_op jit(solution)/shard_map/all_to_all | solution.py:199
  121.6 6.7 %all-to-all-done.2 = f32[2,3,16,4]{3,0,1,2:T(2,128)S(1)} async-done(((f32[2,3,16,4]{3,0,1,2:T(2,128)}), f32[2,3,16,4]{3,0,1,2:T(2,128)S(1)}, u32[]{:S(2)}, u32[]{:S(2)}) %all-to-all-start.2) | async-done | bytes 1568 | tf_op jit(solution)/shard_map/all_to_all | solution.py:199
  130.0 3.2 %all-to-all-start.3 = ((f32[2,1,192]{2,1,0:T(1,128)}), f32[2,1,192]{2,1,0:T(1,128)S(1)}, u32[]{:S(2)}, u32[]{:S(2)}) async-start(f32[2,1,192]{2,1,0:T(1,128)} %reshape.1618), calls=%async_computation.3 | async-start | bytes 4096 | tf_op jit(solution)/shard_map/all_to_all | solution.py:202
  133.8 3.2 %all-to-all-done.3 = f32[2,1,192]{2,1,0:T(1,128)S(1)} async-done(((f32[2,1,192]{2,1,0:T(1,128)}), f32[2,1,192]{2,1,0:T(1,128)S(1)}, u32[]{:S(2)}, u32[]{:S(2)}) %all-to-all-start.3) | async-done | bytes 1568 | tf_op jit(solution)/shard_map/all_to_all | solution.py:202
  138.9 1.1 collective-permute-done.12
  140.1 1.8 %collective-permute-start.14 = (f32[19,6,1,128]{3,2,1,0:T(1,128)S(1)}, f32[19,6,1,128]{3,2,1,0:T(1,128)S(1)}, u32[]{:S(2)}, u32[]{:S(2)}) collective-permute-start(f32[19,6,1,128]{3,2,1,0:T(1,128)S(1)} %get-tuple-element.196), channel_id=1, source_target_pairs={{0,1},{1,0},{2,3},{3,2},{4,5},{5,4},{6,7},{7,6},{8,9},{9,8},{10,11... | collective-permute-start | bytes 175112 | tf_op jit(solution)/shard_map/ppermute | solution.py:47
  142.2 2.2 %collective-permute-done.14 = f32[19,6,1,128]{3,2,1,0:T(1,128)S(1)} collective-permute-done((f32[19,6,1,128]{3,2,1,0:T(1,128)S(1)}, f32[19,6,1,128]{3,2,1,0:T(1,128)S(1)}, u32[]{:S(2)}, u32[]{:S(2)}) %collective-permute-start.14) | collective-permute-done | bytes 58400 | tf_op jit(solution)/shard_map/ppermute | solution.py:47
  144.4 1.7 %collective-permute-done.15 = f32[19,6,1,128]{3,2,1,0:T(1,128)S(1)} collective-permute-done((f32[19,6,1,128]{3,2,1,0:T(1,128)S(1)}, f32[19,6,1,128]{3,2,1,0:T(1,128)S(1)}, u32[]{:S(2)}, u32[]{:S(2)}) %collective-permute-start.15) | collective-permute-done | bytes 58400 | tf_op jit(solution)/shard_map/ppermute | solution.py:49
  (452 shorter events, 67.1 us)
Async XLA Ops:
  0.6 7.3 %copy-start = (f32[19,4,8,128]{3,2,1,0:T(8,128)S(1)}, f32[19,4,8,128]{3,2,1,0:T(8,128)}, u32[]{:S(2)}) copy-start(f32[19,4,8,128]{3,2,1,0:T(8,128)} %param.22) | copy-start | bytes 933892
  10.2 1.1 copy-start.19
  11.3 12.2 %collective-permute-start = (f32[19,1,8,128]{3,2,1,0:T(8,128)S(1)}, f32[19,1,8,128]{3,2,1,0:T(8,128)S(1)}, u32[]{:S(2)}, u32[]{:S(2)}) collective-permute-start(f32[19,1,8,128]{3,2,1,0:T(8,128)S(1)} %get-tuple-element.234), channel_id=1, source_target_pairs={{2,0},{4,2},{6,4},{8,6},{10,8},{12,10},{14,12},{16,14},{18,16},{20... | collective-permute-start | bytes 233480 | tf_op jit(solution)/shard_map/ppermute | solution.py:49
  16.8 6.7 %collective-permute-start.1 = (f32[19,1,8,128]{3,2,1,0:T(8,128)S(1)}, f32[19,1,8,128]{3,2,1,0:T(8,128)S(1)}, u32[]{:S(2)}, u32[]{:S(2)}) collective-permute-start(f32[19,1,8,128]{3,2,1,0:T(8,128)S(1)} %get-tuple-element.235), channel_id=1, source_target_pairs={{0,2},{2,4},{4,6},{6,8},{8,10},{10,12},{12,14},{14,16},{16,18},{18... | collective-permute-start | bytes 233480 | tf_op jit(solution)/shard_map/ppermute | solution.py:47
  23.6 4.3 %collective-permute-start.3 = (f32[19,6,1,128]{3,2,1,0:T(1,128)S(1)}, f32[19,6,1,128]{3,2,1,0:T(1,128)S(1)}, u32[]{:S(2)}, u32[]{:S(2)}) collective-permute-start(f32[19,6,1,128]{3,2,1,0:T(1,128)S(1)} %get-tuple-element.202), channel_id=1, source_target_pairs={{0,1},{1,0},{2,3},{3,2},{4,5},{5,4},{6,7},{7,6},{8,9},{9,8},{10,11... | collective-permute-start | bytes 175112 | tf_op jit(solution)/shard_map/ppermute | solution.py:47
  25.1 4.2 %collective-permute-start.2 = (f32[19,6,1,128]{3,2,1,0:T(1,128)S(1)}, f32[19,6,1,128]{3,2,1,0:T(1,128)S(1)}, u32[]{:S(2)}, u32[]{:S(2)}) collective-permute-start(f32[19,6,1,128]{3,2,1,0:T(1,128)S(1)} %get-tuple-element.201), channel_id=1, source_target_pairs={{1,0},{0,1},{3,2},{2,3},{5,4},{4,5},{7,6},{6,7},{9,8},{8,9},{11,10... | collective-permute-start | bytes 175112 | tf_op jit(solution)/shard_map/ppermute | solution.py:49
  31.6 5.1 %collective-permute-start.4 = (f32[19,1,8,128]{3,2,1,0:T(8,128)S(1)}, f32[19,1,8,128]{3,2,1,0:T(8,128)S(1)}, u32[]{:S(2)}, u32[]{:S(2)}) collective-permute-start(f32[19,1,8,128]{3,2,1,0:T(8,128)S(1)} %get-tuple-element.230), channel_id=1, source_target_pairs={{2,0},{4,2},{6,4},{8,6},{10,8},{12,10},{14,12},{16,14},{18,16},{20... | collective-permute-start | bytes 233480 | tf_op jit(solution)/shard_map/ppermute | solution.py:49
  34.7 6.5 %collective-permute-start.5 = (f32[19,1,8,128]{3,2,1,0:T(8,128)S(1)}, f32[19,1,8,128]{3,2,1,0:T(8,128)S(1)}, u32[]{:S(2)}, u32[]{:S(2)}) collective-permute-start(f32[19,1,8,128]{3,2,1,0:T(8,128)S(1)} %get-tuple-element.231), channel_id=1, source_target_pairs={{0,2},{2,4},{4,6},{6,8},{8,10},{10,12},{12,14},{14,16},{16,18},{18... | collective-permute-start | bytes 233480 | tf_op jit(solution)/shard_map/ppermute | solution.py:47
  41.3 4.3 %collective-permute-start.7 = (f32[19,6,1,128]{3,2,1,0:T(1,128)S(1)}, f32[19,6,1,128]{3,2,1,0:T(1,128)S(1)}, u32[]{:S(2)}, u32[]{:S(2)}) collective-permute-start(f32[19,6,1,128]{3,2,1,0:T(1,128)S(1)} %get-tuple-element.200), channel_id=1, source_target_pairs={{0,1},{1,0},{2,3},{3,2},{4,5},{5,4},{6,7},{7,6},{8,9},{9,8},{10,11... | collective-permute-start | bytes 175112 | tf_op jit(solution)/shard_map/ppermute | solution.py:47
  42.2 4.2 %collective-permute-start.6 = (f32[19,6,1,128]{3,2,1,0:T(1,128)S(1)}, f32[19,6,1,128]{3,2,1,0:T(1,128)S(1)}, u32[]{:S(2)}, u32[]{:S(2)}) collective-permute-start(f32[19,6,1,128]{3,2,1,0:T(1,128)S(1)} %get-tuple-element.199), channel_id=1, source_target_pairs={{1,0},{0,1},{3,2},{2,3},{5,4},{4,5},{7,6},{6,7},{9,8},{8,9},{11,10... | collective-permute-start | bytes 175112 | tf_op jit(solution)/shard_map/ppermute | solution.py:49
  48.7 2.1 %collective-permute-start.8 = (f32[19,1,8,128]{3,2,1,0:T(8,128)S(1)}, f32[19,1,8,128]{3,2,1,0:T(8,128)S(1)}, u32[]{:S(2)}, u32[]{:S(2)}) collective-permute-start(f32[19,1,8,128]{3,2,1,0:T(8,128)S(1)} %get-tuple-element.226), channel_id=1, source_target_pairs={{2,0},{4,2},{6,4},{8,6},{10,8},{12,10},{14,12},{16,14},{18,16},{20... | collective-permute-start | bytes 233480 | tf_op jit(solution)/shard_map/ppermute | solution.py:49
  48.8 6.8 %collective-permute-start.9 = (f32[19,1,8,128]{3,2,1,0:T(8,128)S(1)}, f32[19,1,8,128]{3,2,1,0:T(8,128)S(1)}, u32[]{:S(2)}, u32[]{:S(2)}) collective-permute-start(f32[19,1,8,128]{3,2,1,0:T(8,128)S(1)} %get-tuple-element.227), channel_id=1, source_target_pairs={{0,2},{2,4},{4,6},{6,8},{8,10},{10,12},{12,14},{14,16},{16,18},{18... | collective-permute-start | bytes 233480 | tf_op jit(solution)/shard_map/ppermute | solution.py:47
  55.6 4.3 %collective-permute-start.11 = (f32[19,6,1,128]{3,2,1,0:T(1,128)S(1)}, f32[19,6,1,128]{3,2,1,0:T(1,128)S(1)}, u32[]{:S(2)}, u32[]{:S(2)}) collective-permute-start(f32[19,6,1,128]{3,2,1,0:T(1,128)S(1)} %get-tuple-element.198), channel_id=1, source_target_pairs={{0,1},{1,0},{2,3},{3,2},{4,5},{5,4},{6,7},{7,6},{8,9},{9,8},{10,11... | collective-permute-start | bytes 175112 | tf_op jit(solution)/shard_map/ppermute | solution.py:47
  56.8 4.2 %collective-permute-start.10 = (f32[19,6,1,128]{3,2,1,0:T(1,128)S(1)}, f32[19,6,1,128]{3,2,1,0:T(1,128)S(1)}, u32[]{:S(2)}, u32[]{:S(2)}) collective-permute-start(f32[19,6,1,128]{3,2,1,0:T(1,128)S(1)} %get-tuple-element.197), channel_id=1, source_target_pairs={{1,0},{0,1},{3,2},{2,3},{5,4},{4,5},{7,6},{6,7},{9,8},{8,9},{11,10... | collective-permute-start | bytes 175112 | tf_op jit(solution)/shard_map/ppermute | solution.py:49
  59.9 2.7 %copy-start.21 = (f32[1,4,8,128]{3,2,1,0:T(8,128)}, f32[1,4,8,128]{3,2,1,0:T(8,128)S(1)}, u32[]{:S(2)}) copy-start(f32[1,4,8,128]{3,2,1,0:T(8,128)S(1)} %get-tuple-element.78) | copy-start | bytes 49156
  61.0 1.6 %copy-start.23 = (f32[1,4,8,128]{3,2,1,0:T(8,128)}, f32[1,4,8,128]{3,2,1,0:T(8,128)S(1)}, u32[]{:S(2)}) copy-start(f32[1,4,8,128]{3,2,1,0:T(8,128)S(1)} %get-tuple-element.76) | copy-start | bytes 49156
  61.1 1.5 %copy-start.25 = (f32[4,8,128]{2,1,0:T(8,128)}, f32[4,8,128]{2,1,0:T(8,128)S(1)}, u32[]{:S(2)}) copy-start(f32[4,8,128]{2,1,0:T(8,128)S(1)} %get-tuple-element.74) | copy-start | bytes 49156
  85.3 0.8 copy-start.1
  87.0 0.8 copy-start.3
  93.6 7.0 %all-to-all-start = ((f32[2,1,384]{2,1,0:T(1,128)}), f32[2,1,384]{2,1,0:T(1,128)S(1)}, u32[]{:S(2)}, u32[]{:S(2)}) async-start(f32[2,1,384]{2,1,0:T(1,128)} %reshape.1616), calls=%async_computation | async-start | bytes 6144 | tf_op jit(solution)/shard_map/all_to_all | solution.py:143
  101.7 6.1 %copy-start.38 = (f32[19]{0:T(128)S(1)}, f32[19]{0:T(128)}, u32[]{:S(2)}) copy-start(f32[19]{0:T(128)} %constant.151.clone) | copy-start | bytes 232
  103.8 3.9 %copy-start.20 = (f32[4,8,128]{2,1,0:T(8,128)S(1)}, f32[4,8,128]{2,1,0:T(8,128)}, u32[]{:S(2)}) copy-start(f32[4,8,128]{2,1,0:T(8,128)} %copy-done.19) | copy-start | bytes 49156
  103.8 10.5 %all-to-all-start.1 = ((f32[2,6,1,64]{1,0,2,3:T(2,128)}), f32[2,6,1,64]{1,0,2,3:T(2,128)S(1)}, u32[]{:S(2)}, u32[]{:S(2)}) async-start(f32[2,6,1,64]{1,0,2,3:T(2,128)} %copy.123), calls=%async_computation.1 | async-start | bytes 131072 | tf_op jit(solution)/shard_map/all_to_all | solution.py:148
  108.4 7.1 %copy-start.42 = (f32[16]{0:T(128)S(1)}, f32[16]{0:T(128)}, u32[]{:S(2)}) copy-start(f32[16]{0:T(128)} %get-tuple-element.306) | copy-start | bytes 196
  108.4 7.2 %copy-start.43 = (f32[4]{0:T(128)S(1)}, f32[4]{0:T(128)}, u32[]{:S(2)}) copy-start(f32[4]{0:T(128)} %get-tuple-element.303) | copy-start | bytes 52
  108.4 7.2 %copy-start.44 = (f32[4]{0:T(128)S(1)}, f32[4]{0:T(128)}, u32[]{:S(2)}) copy-start(f32[4]{0:T(128)} %get-tuple-element.304) | copy-start | bytes 52
  118.1 10.2 %all-to-all-start.2 = ((f32[2,3,16,4]{3,0,1,2:T(2,128)}), f32[2,3,16,4]{3,0,1,2:T(2,128)S(1)}, u32[]{:S(2)}, u32[]{:S(2)}) async-start(f32[2,3,16,4]{3,0,1,2:T(2,128)} %copy.128), calls=%async_computation.2 | async-start | bytes 98304 | tf_op jit(solution)/shard_map/all_to_all | solution.py:199
  130.0 7.0 %all-to-all-start.3 = ((f32[2,1,192]{2,1,0:T(1,128)}), f32[2,1,192]{2,1,0:T(1,128)S(1)}, u32[]{:S(2)}, u32[]{:S(2)}) async-start(f32[2,1,192]{2,1,0:T(1,128)} %reshape.1618), calls=%async_computation.3 | async-start | bytes 4096 | tf_op jit(solution)/shard_map/all_to_all | solution.py:202
  133.3 5.7 %collective-permute-start.13 = (f32[19,1,8,128]{3,2,1,0:T(8,128)S(1)}, f32[19,1,8,128]{3,2,1,0:T(8,128)S(1)}, u32[]{:S(2)}, u32[]{:S(2)}) collective-permute-start(f32[19,1,8,128]{3,2,1,0:T(8,128)S(1)} %get-tuple-element.222), channel_id=1, source_target_pairs={{2,0},{4,2},{6,4},{8,6},{10,8},{12,10},{14,12},{16,14},{18,16},{20... | collective-permute-start | bytes 233480 | tf_op jit(solution)/shard_map/ppermute | solution.py:49
  133.5 6.5 %collective-permute-start.12 = (f32[19,1,8,128]{3,2,1,0:T(8,128)S(1)}, f32[19,1,8,128]{3,2,1,0:T(8,128)S(1)}, u32[]{:S(2)}, u32[]{:S(2)}) collective-permute-start(f32[19,1,8,128]{3,2,1,0:T(8,128)S(1)} %get-tuple-element.223), channel_id=1, source_target_pairs={{0,2},{2,4},{4,6},{6,8},{8,10},{10,12},{12,14},{14,16},{16,18},{18... | collective-permute-start | bytes 233480 | tf_op jit(solution)/shard_map/ppermute | solution.py:47
  140.1 4.3 %collective-permute-start.14 = (f32[19,6,1,128]{3,2,1,0:T(1,128)S(1)}, f32[19,6,1,128]{3,2,1,0:T(1,128)S(1)}, u32[]{:S(2)}, u32[]{:S(2)}) collective-permute-start(f32[19,6,1,128]{3,2,1,0:T(1,128)S(1)} %get-tuple-element.196), channel_id=1, source_target_pairs={{0,1},{1,0},{2,3},{3,2},{4,5},{5,4},{6,7},{7,6},{8,9},{9,8},{10,11... | collective-permute-start | bytes 175112 | tf_op jit(solution)/shard_map/ppermute | solution.py:47
  141.9 4.2 %collective-permute-start.15 = (f32[19,6,1,128]{3,2,1,0:T(1,128)S(1)}, f32[19,6,1,128]{3,2,1,0:T(1,128)S(1)}, u32[]{:S(2)}, u32[]{:S(2)}) collective-permute-start(f32[19,6,1,128]{3,2,1,0:T(1,128)S(1)} %get-tuple-element.195), channel_id=1, source_target_pairs={{1,0},{0,1},{3,2},{2,3},{5,4},{4,5},{7,6},{6,7},{9,8},{8,9},{11,10... | collective-permute-start | bytes 175112 | tf_op jit(solution)/shard_map/ppermute | solution.py:49
  (33 other events, 23.3 us)
where the time goes:
time: 150 us; the launch traced here: 148 us
  local copies, waits for them, and re-layouts  53.8 us (36%)
  waiting for transfers between devices  44.8 us (30%)
  starting transfers between devices  31.8 us (21%)
  other arithmetic  11.5 us (8%)
  matrix products  4.31 us (3%)
  between operations  2.24 us (1%)
    another operation x52, local copies, waits for them, and re-layouts, collide(): jnp.stack([moment[first] * moment[later] / density * fluid for first, lat...  26.4 us
    unnamed x188, local copies, waits for them, and re-layouts  21.4 us
    ppermute x8, waiting for transfers between devices, with_halo(): lax.ppermute(tail, axis, [(i, (i + 1) % count) for i in range(count)])  18.9 us
    ppermute x8, starting transfers between devices, with_halo(): lax.ppermute(head, axis, [((i + 1) % count, i) for i in range(count)])  11.7 us
    all_to_all x1, waiting for transfers between devices, local(): lax.all_to_all(jnp.stack([real, imag]), 'gx', split_axis=2, concat_axis=3...  6.71 us
    ppermute x8, waiting for transfers between devices, with_halo(): lax.ppermute(head, axis, [((i + 1) % count, i) for i in range(count)])  6.66 us
    ppermute x8, starting transfers between devices, with_halo(): lax.ppermute(tail, axis, [(i, (i + 1) % count) for i in range(count)])  6.35 us
    all_to_all x1, waiting for transfers between devices, local(): lax.all_to_all(spectrum, 'gx', split_axis=3, concat_axis=2, tiled=True)  5.56 us
  transfers between devices with their start and end apart: 20, of which 17 were waited for; matrix products, arithmetic and copies ran while one was open for 7% of the time, Pallas kernels for 0%

commit v1 on v0

v1 whole, which is shorter than its diff:
```python
import functools
import math

import jax
import jax.numpy as jnp
import numpy as np
from jax import lax
from jax.experimental import pallas as pl
from jax.experimental.pallas import tpu as pltpu
from jax.sharding import PartitionSpec as P

MESH = pl.DeviceIdType.MESH
NZ = 128
STEPS = 4
CUT = 4
VELOCITY = [
    (0, 0, 0),
    (1, 0, 0),
    (-1, 0, 0),
    (0, 1, 0),
    (0, -1, 0),
    (0, 0, 1),
    (0, 0, -1),
    (1, 1, 0),
    (-1, -1, 0),
    (1, -1, 0),
    (-1, 1, 0),
    (1, 0, 1),
    (-1, 0, -1),
    (1, 0, -1),
    (-1, 0, 1),
    (0, 1, 1),
    (0, -1, -1),
    (0, 1, -1),
    (0, -1, 1),
]
WEIGHTS = [1.0 / 3.0] + [1.0 / 18.0] * 6 + [1.0 / 36.0] * 12
SLOW_VISCOSITY = 0.0004
PAIRS = [(0, 0), (1, 1), (2, 2), (0, 1), (0, 2), (1, 2)]
EVEN = 4
CROSS = {
    (axis, sign): [i for i in range(19) if VELOCITY[i][axis] == sign] for axis in (0, 1) for sign in (1, -1)
}
MESSAGES = 8


def wave_table(length):
    index = np.arange(length)
    return 2.0 * np.pi * np.where(index >= (length + 1) // 2, index - length, index) / length


def response(nx, ny, nz):
    waves = np.meshgrid(wave_table(nx), wave_table(ny), wave_table(nz), indexing="ij")
    square = waves[0] ** 2 + waves[1] ** 2 + waves[2] ** 2
    safe = np.where(square > 0, square, 1.0)
    out = np.zeros((3, 6, nx, ny, nz // 2 + 1), np.complex128)
    for c, (p, q) in enumerate(PAIRS):
        force = [np.zeros_like(square) for _ in range(3)]
        force[p] = force[p] + waves[q]
        if p != q:
            force[q] = force[q] + waves[p]
        inner = sum(waves[a] * force[a] for a in range(3))
        for a in range(3):
            gain = np.where(square > 0, (force[a] - waves[a] * inner / safe) / (SLOW_VISCOSITY * safe), 0.0)
            mirror = np.roll(gain[::-1, ::-1, ::-1], (1, 1, 1), (0, 1, 2))
            odd = 0.5 * (gain - mirror)
            out[a, c] = np.fft.ifft2(-1j * odd, axes=(0, 1))[:, :, : nz // 2 + 1]
    return out


def tables(nx, ny):
    slow = NZ // CUT
    half = slow // 2
    green = response(nx, 2 * ny, slow)
    count = nx * ny
    send = np.zeros((count, 12, 2, 4, slow))
    place = {(0, 0): (0, 0), (0, 1): (0, 1), (2, 0): (0, 2), (2, 1): (0, 3), (1, 0): (1, 0), (1, 1): (1, 1)}
    far_x = np.arange(count) // ny
    far_y = np.arange(count) % ny
    for c in range(6):
        for half_y in range(2):
            for (a, to_y), (row, block) in place.items():
                g = green[a, c][far_x, (2 * far_y + to_y - half_y) % (2 * ny)]
                inside = g[:, 1:half]
                if a < 2:
                    inside = inside.real if c < EVEN else inside.imag
                else:
                    inside = inside.imag if c < EVEN else -inside.real
                send[:, 2 * c + half_y, row, block, : half + 1] = g.real
                send[:, 2 * c + half_y, row, block, 1:half] = inside
                send[:, 2 * c + half_y, row, block, half + 1 :] = inside
    send = send.reshape(count // 4, 4, 12, 2, NZ).transpose(0, 2, 1, 3, 4).reshape(count // 4, 12, 8, NZ)
    place_z = np.arange(slow)
    angle = 2.0 * np.pi * place_z[:, None] * np.arange(half + 1)[None, :] / slow
    cosine, sine = np.cos(angle), np.sin(angle)
    plain = np.concatenate([cosine, -sine[:, 1:half]], axis=1)
    turned = np.concatenate([cosine[:, :1], sine[:, 1:half], cosine[:, half:], cosine[:, 1:half]], axis=1)
    scale = 1.0 / (STEPS * CUT**3)
    forward = np.concatenate([np.tile(plain, (CUT, 1, 4)).reshape(CUT, slow, NZ).transpose(1, 0, 2).reshape(NZ, NZ),
                              np.tile(turned, (CUT, 1, 4)).reshape(CUT, slow, NZ).transpose(1, 0, 2).reshape(NZ, NZ)], axis=1)
    forward = forward * scale
    edge = [cosine[:, :1], cosine[:, half:]]
    back = np.concatenate([edge[0], 2 * cosine[:, 1:half], edge[1], -2 * sine[:, 1:half]], axis=1).T / slow
    back_turned = np.concatenate([edge[0], -2 * sine[:, 1:half], edge[1], -2 * cosine[:, 1:half]], axis=1).T / slow
    inverse = np.concatenate([back, back, back_turned, back_turned], axis=0)
    inverse = np.concatenate([inverse, np.zeros((NZ, NZ - slow))], axis=1)
    return send.astype(np.float32), forward.astype(np.float32), inverse.astype(np.float32)


def dot(left, right):
    return jnp.dot(left, right, precision=lax.Precision.HIGHEST, preferred_element_type=jnp.float32)


def moments(f):
    rho = f[0]
    for i in range(1, 19):
        rho = rho + f[i]
    j = []
    for axis in range(3):
        plus = [f[i] for i in range(19) if VELOCITY[i][axis] == 1]
        minus = [f[i] for i in range(19) if VELOCITY[i][axis] == -1]
        total = plus[0] - minus[0]
        for one, other in zip(plus[1:], minus[1:]):
            total = total + (one - other)
        j.append(total)
    return rho, j


def collide(f, rho, j, inverse, keep, omega, push, solid):
    speed = [one * inverse for one in j]
    square = speed[0] * speed[0] + speed[1] * speed[1] + speed[2] * speed[2]
    weight = omega * rho
    base = weight * (1.0 - 1.5 * square)
    quad = 4.5 * weight
    lead = [3.0 * (omega * j[a] + push[a]) for a in range(3)]
    post = [None] * 19
    post[0] = jnp.where(solid, f[0], keep * f[0] + WEIGHTS[0] * base)
    for i in range(1, 19, 2):
        along = linear = None
        for axis in range(3):
            c = VELOCITY[i][axis]
            if c:
                along = c * speed[axis] if along is None else along + speed[axis] if c > 0 else along - speed[axis]
                linear = c * lead[axis] if linear is None else linear + lead[axis] if c > 0 else linear - lead[axis]
        even = WEIGHTS[i] * (base + quad * (along * along))
        odd = WEIGHTS[i] * linear
        post[i] = jnp.where(solid, f[i + 1], keep * f[i] + (even + odd))
        post[i + 1] = jnp.where(solid, f[i], keep * f[i + 1] + (even - odd))
    return post


def kernel(
    nx, ny, pops_hbm, label_hbm, drive_hbm, table_hbm, forward_hbm, inverse_hbm, momentum_hbm, running_ref,
    state, label, drive, table, forward, inverse_z, momentum, face_out, face_in, row_out, row_in, edge_out, edge_in,
    message, arrived, load_sem, const_sem, halo_send, halo_recv, slow_send, slow_recv, out_sem,
):
    width = label.shape[0]
    gx = lax.axis_index("gx")
    gy = lax.axis_index("gy")
    count = nx * ny

    loads = [
        pltpu.make_async_copy(pops_hbm, state.at[0], load_sem.at[0]),
        pltpu.make_async_copy(label_hbm, label, load_sem.at[1]),
        pltpu.make_async_copy(drive_hbm, drive, load_sem.at[2]),
    ]
    constants = [
        pltpu.make_async_copy(table_hbm, table, const_sem.at[0]),
        pltpu.make_async_copy(forward_hbm, forward, const_sem.at[1]),
        pltpu.make_async_copy(inverse_hbm, inverse_z, const_sem.at[2]),
    ]
    for copy in loads + constants:
        copy.start()

    def device_at(far):
        return (lax.rem(gx + far // ny, nx), lax.rem(gy + far % ny, ny))

    def over_others(body):
        if count <= 64:
            for far in range(1, count):
                body(far)
        else:
            def step(far, carry):
                body(far)
                return carry

            lax.fori_loop(1, count, step, 0)

    barrier = pltpu.get_barrier_semaphore()
    over_others(lambda far: pl.semaphore_signal(barrier, inc=1, device_id=device_at(far), device_id_type=MESH))

    for copy in loads:
        copy.wait()

    east, west = lax.rem(gx + 1, nx), lax.rem(gx + nx - 1, nx)
    north, south = lax.rem(gy + 1, ny), lax.rem(gy + ny - 1, ny)
    side_x = {1: east, -1: west}
    side_y = {1: north, -1: south}
    slot = {1: 0, -1: 1}

    def remote(src, dst, step, number, place):
        return pltpu.make_async_remote_copy(
            src_ref=src,
            dst_ref=dst,
            send_sem=halo_send.at[step, number],
            recv_sem=halo_recv.at[step, number],
            device_id=place,
            device_id_type=MESH,
        )

    def halo(step):
        copies = []
        for sign in (1, -1):
            s = slot[sign]
            copies.append(remote(face_out.at[step, s], face_in.at[step, s], step, s, (side_x[sign], gy)))
        if ny == 2:
            copies.append(remote(row_out.at[step], row_in.at[step], step, 2, (gx, north)))
            for sign in (1, -1):
                s = slot[sign]
                copies.append(remote(edge_out.at[step, s], edge_in.at[step, s], step, 4 + s, (side_x[sign], north)))
        else:
            for sign in (1, -1):
                s = slot[sign]
                copies.append(remote(row_out.at[step, s], row_in.at[step, s], step, 2 + s, (gx, side_y[sign])))
                for turn in (1, -1):
                    t = slot[turn]
                    copies.append(
                        remote(
                            edge_out.at[step, t, s], edge_in.at[step, t, s], step, 4 + 2 * t + s,
                            (side_x[turn], side_y[sign]),
                        )
                    )
        return copies

    row_id = lax.broadcasted_iota(jnp.int32, (8, NZ), 0)
    first_row = row_id == 0
    last_row = row_id == 7

    def read(step, i, p):
        cx, cy, _ = VELOCITY[i]
        if step == 0:
            return state[0, i, p]
        outside = (cx == 1 and p == 0) or (cx == -1 and p == width - 1)
        if outside:
            value = face_in[step - 1, slot[cx], CROSS[0, cx].index(i)]
        else:
            value = state[step % 2, i, p]
        if cy:
            if outside:
                row = edge_in[step - 1, slot[cx], slot[cy]]
            else:
                row = row_in[step - 1, slot[cy], CROSS[1, cy].index(i) * width + p]
            value = jnp.where(first_row if cy == 1 else last_row, jnp.broadcast_to(row, (8, NZ)), value)
        return value

    def write(step, i, p, value):
        cx, cy, cz = VELOCITY[i]
        if cz:
            value = pltpu.roll(value, cz % NZ, 1)
        if cy:
            value = pltpu.roll(value, cy % 8, 0)
            line = value[0:1] if cy == 1 else value[7:8]
        outside = (cx == 1 and p == width - 1) or (cx == -1 and p == 0)
        if outside:
            face_out[step, slot[cx], CROSS[0, cx].index(i)] = value
            if cy:
                edge_out[step, slot[cx], slot[cy]] = line
        else:
            state[(step + 1) % 2, i, p + cx] = value
            if cy:
                row_out[step, slot[cy], CROSS[1, cy].index(i) * width + p + cx] = line

    def send_copy(far):
        return pltpu.make_async_remote_copy(
            src_ref=message.at[far],
            dst_ref=arrived.at[far],
            send_sem=slow_send,
            recv_sem=slow_recv,
            device_id=device_at(far),
            device_id_type=MESH,
        )

    total = [None] * 6
    copies = []
    for step in range(STEPS):
        phase = math.cos(2.0 * math.pi * (step + 0.5) / STEPS)
        if step:
            for copy in copies:
                copy.wait_recv()
        held = []
        for p in range(width):
            f = [read(step, i, p) for i in range(19)]
            rho, j = moments(f)
            inverse = 1.0 / rho
            kind = label[p]
            solid = kind == 2
            thin = jnp.where(solid, 0.0, inverse)
            scaled = [one * thin for one in j]
            for c, (a, b) in enumerate(PAIRS):
                term = scaled[a] * j[b]
                total[c] = term if total[c] is None else total[c] + term
            if step == STEPS - 1:
                held.append((rho, j, inverse))
                continue
            second = kind == 1
            omega = jnp.where(second, 1.1, 1.6)
            strength = jnp.where(second, 0.6 * phase, phase)
            push = [strength * drive[a, p] for a in range(3)]
            post = collide(f, rho, j, inverse, 1.0 - omega, omega, push, solid)
            for i in range(19):
                write(step, i, p, post[i])
        if step == STEPS - 1:
            for copy in constants:
                copy.wait()
            plain = dot(jnp.concatenate(total[:EVEN], axis=0), forward[:, :NZ])
            turned = dot(jnp.concatenate(total[EVEN:], axis=0), forward[:, NZ:])
            lines = []
            for c in range(6):
                source = plain if c < EVEN else turned
                tile = source[8 * c : 8 * c + 8] if c < EVEN else source[8 * (c - EVEN) : 8 * (c - EVEN) + 8]
                tile = tile + pltpu.roll(tile, 7, 0)
                tile = tile + pltpu.roll(tile, 6, 0)
                lines.append(jnp.broadcast_to(tile[0:1], (8, NZ)))
                lines.append(jnp.broadcast_to(tile[4:5], (8, NZ)))

            def group(g):
                value = lines[0] * table[g, 0]
                for k in range(1, 12):
                    value = value + lines[k] * table[g, k]
                for k in range(4):
                    message[4 * g + k] = value[2 * k : 2 * k + 2]

            if count <= 64:
                for g in range(count // 4):
                    group(g)
            else:
                def each(g, carry):
                    group(g)
                    return carry

                lax.fori_loop(0, count // 4, each, 0)
            over_others(lambda far: send_copy(far).start())
            for p in range(width):
                f = [read(step, i, p) for i in range(19)]
                rho, j, inverse = held[p]
                kind = label[p]
                second = kind == 1
                omega = jnp.where(second, 1.1, 1.6)
                strength = jnp.where(second, 0.6 * phase, phase)
                push = [strength * drive[a, p] for a in range(3)]
                post = collide(f, rho, j, inverse, 1.0 - omega, omega, push, kind == 2)
                for i in range(19):
                    write(step, i, p, post[i])
        elif step == 0:
            pl.semaphore_wait(barrier, count - 1)
        for copy in copies:
            copy.wait_send()
        copies = halo(step)
        for copy in copies:
            copy.start()

    for copy in copies:
        copy.wait_recv()
    for p in range(width):
        f = [None] + [read(STEPS, i, p) for i in range(1, 19)]
        for axis in range(3):
            value = None
            for i in range(1, 19):
                c = VELOCITY[i][axis]
                if c:
                    value = c * f[i] if value is None else value + f[i] if c > 0 else value - f[i]
            momentum[axis, p] = value
    out_copy = pltpu.make_async_copy(momentum, momentum_hbm, out_sem)
    out_copy.start()
    for copy in copies:
        copy.wait_send()

    rest = pl.ds(1, count - 1)
    pltpu.make_async_copy(message.at[rest], arrived.at[rest], slow_recv).wait()
    spectrum = message[0]
    if count <= 64:
        for far in range(1, count):
            spectrum = spectrum + arrived[far]
    else:
        spectrum = lax.fori_loop(1, count, lambda far, value: value + arrived[far], spectrum)
    upper = jnp.broadcast_to(spectrum[0:1], (8, NZ))
    lower = jnp.broadcast_to(spectrum[1:2], (8, NZ))
    lane = lax.broadcasted_iota(jnp.int32, (8, NZ), 1)
    slow_z = NZ // CUT
    block = row_id % 2 + jnp.where(row_id >= 4, 2, 0)
    low = slow_z * block
    spread = jnp.where((row_id == 2) | (row_id == 3), lower, upper)
    spread = jnp.where((lane >= low) & (lane < low + slow_z), spread, 0.0)
    result = dot(spread, inverse_z[...])
    for a in range(3):
        running_ref[a, 0] = result[2 * a : 2 * a + 2, :slow_z]
    pltpu.make_async_copy(arrived.at[rest], message.at[rest], slow_send).wait()
    out_copy.wait()


def local(nx, ny, constants, pops, label, drive):
    width, height = pops.shape[1], pops.shape[2]
    count = nx * ny
    send, forward, inverse = constants
    anywhere = pl.BlockSpec(memory_space=pl.ANY)
    f32 = jnp.float32
    return pl.pallas_call(
        functools.partial(kernel, nx, ny),
        out_shape=(
            jax.ShapeDtypeStruct((3, width, height, NZ), f32),
            jax.ShapeDtypeStruct((3, width // CUT, height // CUT, NZ // CUT), f32),
        ),
        in_specs=[anywhere] * 6,
        out_specs=(anywhere, pl.BlockSpec(memory_space=pltpu.VMEM)),
        scratch_shapes=[
            pltpu.VMEM((2, 19, width, height, NZ), f32),
            pltpu.VMEM((width, height, NZ), jnp.int32),
            pltpu.VMEM((3, width, height, NZ), f32),
            pltpu.VMEM(send.shape, f32),
            pltpu.VMEM(forward.shape, f32),
            pltpu.VMEM(inverse.shape, f32),
            pltpu.VMEM((3, width, height, NZ), f32),
            pltpu.VMEM((STEPS, 2, 5, height, NZ), f32),
            pltpu.VMEM((STEPS, 2, 5, height, NZ), f32),
            pltpu.VMEM((STEPS, 2, 5 * width, 1, NZ), f32),
            pltpu.VMEM((STEPS, 2, 5 * width, 1, NZ), f32),
            pltpu.VMEM((STEPS, 2, 2, 1, NZ), f32),
            pltpu.VMEM((STEPS, 2, 2, 1, NZ), f32),
            pltpu.VMEM((count, 2, NZ), f32),
            pltpu.VMEM((count, 2, NZ), f32),
            pltpu.SemaphoreType.DMA((3,)),
            pltpu.SemaphoreType.DMA((3,)),
            pltpu.SemaphoreType.DMA((STEPS, MESSAGES)),
            pltpu.SemaphoreType.DMA((STEPS, MESSAGES)),
            pltpu.SemaphoreType.DMA,
            pltpu.SemaphoreType.DMA,
            pltpu.SemaphoreType.DMA,
        ],
        compiler_params=pltpu.CompilerParams(
            collective_id=0, has_side_effects=True, vmem_limit_bytes=32 * 1024 * 1024
        ),
        name="cycle",
    )(pops, label, drive, send, forward, inverse)


def solution(mesh):
    nx, ny = mesh.shape["gx"], mesh.shape["gy"]
    constants = tuple(jnp.asarray(table) for table in tables(nx, ny))
    in_specs = (P(None, "gx", "gy", None), P("gx", "gy", None), P(None, "gx", "gy", None))
    out_specs = (P(None, "gx", "gy", None), P(None, "gx", "gy", None))
    return jax.shard_map(
        functools.partial(local, nx, ny, constants),
        mesh=mesh, in_specs=in_specs, out_specs=out_specs, check_vma=False,
    )
```

time: 150 us -> 33.7 us (0.22)
  local copies, waits for them, and re-layouts: 53.8 us -> 6.42 us
  waiting for transfers between devices: 44.8 us -> 0 us
  starting transfers between devices: 31.8 us -> 0 us
  Pallas kernels: 0 us -> 26.3 us
  other arithmetic: 11.5 us -> 0 us
  matrix products: 4.31 us -> 0 us
  between operations: 2.24 us -> 0.65 us
    another operation x64 -> x0, local copies, waits for them, and re-layouts: 28.3 us -> none  [the longest x52 26.4 us: collide(): jnp.stack([moment[first] * moment[later] / density * fluid for first, lat...]
    pallas_call x0 -> x1, Pallas kernels: none -> 26.3 us  [local(): pl.pallas_call(functools.partial(kernel, nx, ny), out_shape=(jax.ShapeDty...]
    ppermute x16 -> x0, waiting for transfers between devices: 25.6 us -> none  [the longest x8 18.9 us: with_halo(): lax.ppermute(tail, axis, [(i, (i + 1) % count) for i in range(count)])]
    all_to_all x4 -> x0, waiting for transfers between devices: 19.2 us -> none  [the longest x1 6.71 us: local(): lax.all_to_all(jnp.stack([real, imag]), 'gx', split_axis=2, concat_axis=3...]
    ppermute x16 -> x0, starting transfers between devices: 18 us -> none  [the longest x8 11.7 us: with_halo(): lax.ppermute(head, axis, [((i + 1) % count, i) for i in range(count)])]
    unnamed x188 -> x14, local copies, waits for them, and re-layouts: 21.4 us -> 6.42 us
    all_to_all x4 -> x0, starting transfers between devices: 13.8 us -> none  [the longest x1 3.85 us: local(): lax.all_to_all(spectrum, 'gx', split_axis=3, concat_axis=2, tiled=True)]
    dot_general x20 -> x0, matrix products: 4.31 us -> none  [product(): return jnp.matmul(values, table, precision=lax.Precision.HIGHEST)]
  transfers between devices with their start and end apart: 20 -> 0, of which waited for: 17 -> 0; matrix products, arithmetic and copies ran while one was open for 7% -> 0% of each run, Pallas kernels for 0% -> 0%
where the time goes in v1:
time: 33.7 us; the launch traced here: 33.4 us
  Pallas kernels  26.3 us (78%)
  local copies, waits for them, and re-layouts  6.42 us (19%)
  between operations  0.65 us (2%)
    pallas_call x1, Pallas kernels, local(): pl.pallas_call(functools.partial(kernel, nx, ny), out_shape=(jax.ShapeDty...  26.3 us
    unnamed x14, local copies, waits for them, and re-layouts  6.42 us

profile of v1, /device:TPU:0, one launch (start us, length us, event | category | flops | bytes accessed | tf_op | source)
XLA Modules:
  0.0 33.4 jit_solution(6532215890340116107)
XLA Ops:
  0.6 0.0 copy-start
  0.6 1.0 %copy-done = f32[8,12,8,128]{3,2,1,0:T(8,128)S(1)} copy-done((f32[8,12,8,128]{3,2,1,0:T(8,128)S(1)}, f32[8,12,8,128]{3,2,1,0:T(8,128)}, u32[]{:S(2)}) %copy-start) | copy-done | bytes 393240
  1.6 0.0 copy-start.1
  1.6 1.0 %copy-done.1 = f32[19,4,8,128]{3,2,1,0:T(8,128)S(1)} copy-done((f32[19,4,8,128]{3,2,1,0:T(8,128)S(1)}, f32[19,4,8,128]{3,2,1,0:T(8,128)}, u32[]{:S(2)}) %copy-start.1) | copy-done | bytes 311320
  2.6 0.0 copy-start.2
  2.6 0.9 %copy-done.2 = f32[128,256]{1,0:T(8,128)S(1)} copy-done((f32[128,256]{1,0:T(8,128)S(1)}, f32[128,256]{1,0:T(8,128)}, u32[]{:S(2)}) %copy-start.2) | copy-done | bytes 131096
  3.5 0.0 copy-start.3
  3.5 0.8 %copy-done.3 = f32[128,128]{1,0:T(8,128)S(1)} copy-done((f32[128,128]{1,0:T(8,128)S(1)}, f32[128,128]{1,0:T(8,128)}, u32[]{:S(2)}) %copy-start.3) | copy-done | bytes 65560
  4.3 0.0 copy-start.4
  4.3 0.8 %copy-done.4 = f32[3,4,8,128]{3,2,1,0:T(8,128)S(1)} copy-done((f32[3,4,8,128]{3,2,1,0:T(8,128)S(1)}, f32[3,4,8,128]{3,2,1,0:T(8,128)}, u32[]{:S(2)}) %copy-start.4) | copy-done | bytes 49176
  5.1 0.0 copy-start.5
  5.1 0.7 %copy-done.5 = s32[4,8,128]{2,1,0:T(8,128)S(1)} copy-done((s32[4,8,128]{2,1,0:T(8,128)S(1)}, s32[4,8,128]{2,1,0:T(8,128)}, u32[]{:S(2)}) %copy-start.5) | copy-done | bytes 16408
  5.9 26.3 %cycle.1 = (f32[3,4,8,128]{3,2,1,0:T(8,128)S(1)}, f32[3,1,2,32]{3,2,1,0:T(2,128)S(1)}) custom-call(f32[19,4,8,128]{3,2,1,0:T(8,128)S(1)} %copy-done.1, s32[4,8,128]{2,1,0:T(8,128)S(1)} %copy-done.5, f32[3,4,8,128]{3,2,1,0:T(8,128)S(1)} %copy-done.4, f32[8,12,8,128]{3,2,1,0:T(8,128)S(1)} %copy-done, f32[128,256]{1,0:T(8,128)S(1)} %copy-done.2, ...), custom_call_target="tpu_custom_call" | custom-call | tf_op jit(solution)/shard_map/cycle/pallas_call | solution.py:407
  32.2 0.6 %copy.10 = f32[3,4,8,128]{3,2,1,0:T(8,128)} copy(f32[3,4,8,128]{3,2,1,0:T(8,128)S(1)} %get-tuple-element.4) | data formatting | bytes 98304
  32.8 0.6 %copy.11 = f32[3,1,2,32]{3,2,1,0:T(2,128)} copy(f32[3,1,2,32]{3,2,1,0:T(2,128)S(1)} %get-tuple-element.5) | data formatting | bytes 1536
Async XLA Ops:
  0.6 1.0 %copy-start = (f32[8,12,8,128]{3,2,1,0:T(8,128)S(1)}, f32[8,12,8,128]{3,2,1,0:T(8,128)}, u32[]{:S(2)}) copy-start(f32[8,12,8,128]{3,2,1,0:T(8,128)} %constant.6.clone.table_hbm) | copy-start | bytes 1179652
  1.6 1.0 %copy-start.1 = (f32[19,4,8,128]{3,2,1,0:T(8,128)S(1)}, f32[19,4,8,128]{3,2,1,0:T(8,128)}, u32[]{:S(2)}) copy-start(f32[19,4,8,128]{3,2,1,0:T(8,128)} %pops_hbm.1) | copy-start | bytes 933892
  2.6 0.9 %copy-start.2 = (f32[128,256]{1,0:T(8,128)S(1)}, f32[128,256]{1,0:T(8,128)}, u32[]{:S(2)}) copy-start(f32[128,256]{1,0:T(8,128)} %constant.7.clone.forward_hbm) | copy-start | bytes 393220
  3.5 0.8 %copy-start.3 = (f32[128,128]{1,0:T(8,128)S(1)}, f32[128,128]{1,0:T(8,128)}, u32[]{:S(2)}) copy-start(f32[128,128]{1,0:T(8,128)} %constant.8.clone.inverse_hbm) | copy-start | bytes 196612
  4.3 0.8 %copy-start.4 = (f32[3,4,8,128]{3,2,1,0:T(8,128)S(1)}, f32[3,4,8,128]{3,2,1,0:T(8,128)}, u32[]{:S(2)}) copy-start(f32[3,4,8,128]{3,2,1,0:T(8,128)} %drive_hbm.1) | copy-start | bytes 147460
  5.1 0.7 %copy-start.5 = (s32[4,8,128]{2,1,0:T(8,128)S(1)}, s32[4,8,128]{2,1,0:T(8,128)}, u32[]{:S(2)}) copy-start(s32[4,8,128]{2,1,0:T(8,128)} %label_hbm.1) | copy-start | bytes 49156

commit v2 on v1

--- a/solution.py
+++ b/solution.py
@@ -209,28 +209,28 @@
         )
 
     def halo(step):
-        copies = []
+        faces, rows = [], []
         for sign in (1, -1):
             s = slot[sign]
-            copies.append(remote(face_out.at[step, s], face_in.at[step, s], step, s, (side_x[sign], gy)))
+            faces.append(remote(face_out.at[step, s], face_in.at[step, s], step, s, (side_x[sign], gy)))
         if ny == 2:
-            copies.append(remote(row_out.at[step], row_in.at[step], step, 2, (gx, north)))
             for sign in (1, -1):
                 s = slot[sign]
-                copies.append(remote(edge_out.at[step, s], edge_in.at[step, s], step, 4 + s, (side_x[sign], north)))
+                faces.append(remote(edge_out.at[step, s], edge_in.at[step, s], step, 4 + s, (side_x[sign], north)))
+            rows.append(remote(row_out.at[step], row_in.at[step], step, 2, (gx, north)))
         else:
             for sign in (1, -1):
                 s = slot[sign]
-                copies.append(remote(row_out.at[step, s], row_in.at[step, s], step, 2 + s, (gx, side_y[sign])))
                 for turn in (1, -1):
                     t = slot[turn]
-                    copies.append(
+                    faces.append(
                         remote(
                             edge_out.at[step, t, s], edge_in.at[step, t, s], step, 4 + 2 * t + s,
                             (side_x[turn], side_y[sign]),
                         )
                     )
-        return copies
+                rows.append(remote(row_out.at[step, s], row_in.at[step, s], step, 2 + s, (gx, side_y[sign])))
+        return faces, rows
 
     row_id = lax.broadcasted_iota(jnp.int32, (8, NZ), 0)
     first_row = row_id == 0
@@ -281,85 +281,85 @@
         )
 
     total = [None] * 6
-    copies = []
+
+    def advance(step, p):
+        phase = math.cos(2.0 * math.pi * (step + 0.5) / STEPS)
+        f = [read(step, i, p) for i in range(19)]
+        rho, j = moments(f)
+        inverse = 1.0 / rho
+        kind = label[p]
+        solid = kind == 2
+        thin = jnp.where(solid, 0.0, inverse)
+        scaled = [one * thin for one in j]
+        for c, (a, b) in enumerate(PAIRS):
+            term = scaled[a] * j[b]
+            total[c] = term if total[c] is None else total[c] + term
+        second = kind == 1
+        omega = jnp.where(second, 1.1, 1.6)
+        strength = jnp.where(second, 0.6 * phase, phase)
+        push = [strength * drive[a, p] for a in range(3)]
+        post = collide(f, rho, j, inverse, 1.0 - omega, omega, push, solid)
+        for i in range(19):
+            write(step, i, p, post[i])
+
+    outer = [0, width - 1]
+    inner = list(range(1, width - 1))
+    started = []
     for step in range(STEPS):
-        phase = math.cos(2.0 * math.pi * (step + 0.5) / STEPS)
-        if step:
-            for copy in copies:
+        if step == 0:
+            for p in outer:
+                advance(step, p)
+            pl.semaphore_wait(barrier, count - 1)
+        else:
+            for copy in rows:
                 copy.wait_recv()
-        held = []
-        for p in range(width):
-            f = [read(step, i, p) for i in range(19)]
-            rho, j = moments(f)
-            inverse = 1.0 / rho
-            kind = label[p]
-            solid = kind == 2
-            thin = jnp.where(solid, 0.0, inverse)
-            scaled = [one * thin for one in j]
-            for c, (a, b) in enumerate(PAIRS):
-                term = scaled[a] * j[b]
-                total[c] = term if total[c] is None else total[c] + term
-            if step == STEPS - 1:
-                held.append((rho, j, inverse))
-                continue
-            second = kind == 1
-            omega = jnp.where(second, 1.1, 1.6)
-            strength = jnp.where(second, 0.6 * phase, phase)
-            push = [strength * drive[a, p] for a in range(3)]
-            post = collide(f, rho, j, inverse, 1.0 - omega, omega, push, solid)
-            for i in range(19):
-                write(step, i, p, post[i])
-        if step == STEPS - 1:
-            for copy in constants:
-                copy.wait()
-            plain = dot(jnp.concatenate(total[:EVEN], axis=0), forward[:, :NZ])
-            turned = dot(jnp.concatenate(total[EVEN:], axis=0), forward[:, NZ:])
-            lines = []
-            for c in range(6):
-                source = plain if c < EVEN else turned
-                tile = source[8 * c : 8 * c + 8] if c < EVEN else source[8 * (c - EVEN) : 8 * (c - EVEN) + 8]
-                tile = tile + pltpu.roll(tile, 7, 0)
-                tile = tile + pltpu.roll(tile, 6, 0)
-                lines.append(jnp.broadcast_to(tile[0:1], (8, NZ)))
-                lines.append(jnp.broadcast_to(tile[4:5], (8, NZ)))
-
-            def group(g):
-                value = lines[0] * table[g, 0]
-                for k in range(1, 12):
-                    value = value + lines[k] * table[g, k]
-                for k in range(4):
-                    message[4 * g + k] = value[2 * k : 2 * k + 2]
-
-            if count <= 64:
-                for g in range(count // 4):
-                    group(g)
-            else:
-                def each(g, carry):
-                    group(g)
-                    return carry
-
-                lax.fori_loop(0, count // 4, each, 0)
-            over_others(lambda far: send_copy(far).start())
-            for p in range(width):
-                f = [read(step, i, p) for i in range(19)]
-                rho, j, inverse = held[p]
-                kind = label[p]
-                second = kind == 1
-                omega = jnp.where(second, 1.1, 1.6)
-                strength = jnp.where(second, 0.6 * phase, phase)
-                push = [strength * drive[a, p] for a in range(3)]
-                post = collide(f, rho, j, inverse, 1.0 - omega, omega, push, kind == 2)
-                for i in range(19):
-                    write(step, i, p, post[i])
-        elif step == 0:
-            pl.semaphore_wait(barrier, count - 1)
-        for copy in copies:
-            copy.wait_send()
-        copies = halo(step)
-        for copy in copies:
+            for p in inner:
+                advance(step, p)
+            for copy in faces:
+                copy.wait_recv()
+            for p in outer:
+                advance(step, p)
+        faces, rows = halo(step)
+        started += faces + rows
+        for copy in faces:
             copy.start()
-
-    for copy in copies:
+        if step == 0:
+            for p in inner:
+                advance(step, p)
+        for copy in rows:
+            copy.start()
+
+    for copy in constants:
+        copy.wait()
+    plain = dot(jnp.concatenate(total[:EVEN], axis=0), forward[:, :NZ])
+    turned = dot(jnp.concatenate(total[EVEN:], axis=0), forward[:, NZ:])
+    lines = []
+    for c in range(6):
+        tile = plain[8 * c : 8 * c + 8] if c < EVEN else turned[8 * (c - EVEN) : 8 * (c - EVEN) + 8]
+        tile = tile + pltpu.roll(tile, 7, 0)
+        tile = tile + pltpu.roll(tile, 6, 0)
+        lines.append(jnp.broadcast_to(tile[0:1], (8, NZ)))
+        lines.append(jnp.broadcast_to(tile[4:5], (8, NZ)))
+
+    def group(g):
+        value = lines[0] * table[g, 0]
+        for k in range(1, 12):
+            value = value + lines[k] * table[g, k]
+        for k in range(4):
+            message[4 * g + k] = value[2 * k : 2 * k + 2]
+
+    if count <= 64:
+        for g in range(count // 4):
+            group(g)
+    else:
+        def each(g, carry):
+            group(g)
+            return carry
+
+        lax.fori_loop(0, count // 4, each, 0)
+    over_others(lambda far: send_copy(far).start())
+
+    for copy in faces + rows:
         copy.wait_recv()
     for p in range(width):
         f = [None] + [read(STEPS, i, p) for i in range(1, 19)]
@@ -372,7 +372,7 @@
             momentum[axis, p] = value
     out_copy = pltpu.make_async_copy(momentum, momentum_hbm, out_sem)
     out_copy.start()
-    for copy in copies:
+    for copy in started:
         copy.wait_send()
 
     rest = pl.ds(1, count - 1)
@@ -402,7 +402,7 @@
     width, height = pops.shape[1], pops.shape[2]
     count = nx * ny
     send, forward, inverse = constants
-    anywhere = pl.BlockSpec(memory_space=pl.ANY)
+    anywhere = pl.BlockSpec(memory_space=pltpu.HBM)
     f32 = jnp.float32
     return pl.pallas_call(
         functools.partial(kernel, nx, ny),
@@ -437,7 +437,7 @@
             pltpu.SemaphoreType.DMA,
         ],
         compiler_params=pltpu.CompilerParams(
-            collective_id=0, has_side_effects=True, vmem_limit_bytes=32 * 1024 * 1024
+            collective_id=0, has_side_effects=True, vmem_limit_bytes=60 * 1024 * 1024
         ),
         name="cycle",
     )(pops, label, drive, send, forward, inverse)

time: 33.7 us -> 28.7 us (0.85)
  local copies, waits for them, and re-layouts: 6.42 us -> 2 us
  Pallas kernels: 26.3 us -> 25.9 us
    unnamed x14 -> x4, local copies, waits for them, and re-layouts: 6.42 us -> 2 us
    pallas_call x1, Pallas kernels: 26.3 us -> 25.9 us  [local(): pl.pallas_call(functools.partial(kernel, nx, ny), out_shape=(jax.ShapeDty...]
where the time goes in v2:
time: 28.7 us; the launch traced here: 28.5 us
  Pallas kernels  25.9 us (90%)
  local copies, waits for them, and re-layouts  2 us (7%)
  between operations  0.65 us (2%)
    pallas_call x1, Pallas kernels, local(): pl.pallas_call(functools.partial(kernel, nx, ny), out_shape=(jax.ShapeDty...  25.9 us
    unnamed x4, local copies, waits for them, and re-layouts  2 us

profile of v2, /device:TPU:0, one launch (start us, length us, event | category | flops | bytes accessed | tf_op | source)
XLA Modules:
  0.0 28.5 jit_solution(10220894712587304741)
XLA Ops:
  0.6 25.9 %cycle.1 = (f32[3,4,8,128]{3,2,1,0:T(8,128)}, f32[3,1,2,32]{3,2,1,0:T(2,128)}) custom-call(f32[19,4,8,128]{3,2,1,0:T(8,128)} %pops_hbm.1, s32[4,8,128]{2,1,0:T(8,128)} %label_hbm.1, f32[3,4,8,128]{3,2,1,0:T(8,128)} %drive_hbm.1, f32[8,12,8,128]{3,2,1,0:T(8,128)} %constant.6.clone.table_hbm, f32[128,256]{1,0:T(8,128)} %constant.7.clone.forward_hbm, ...), custom_call_target="tpu_custom_call" | custom-call | tf_op jit(solution)/shard_map/cycle/pallas_call | solution.py:407
  26.5 0.0 copy-start
  26.5 1.4 %copy.10 = f32[3,4,8,128]{3,2,1,0:T(8,128)} copy(f32[3,4,8,128]{3,2,1,0:T(8,128)} %get-tuple-element.4) | data formatting | bytes 98304
  28.0 0.0 copy-done
  28.0 0.6 %copy.11 = f32[3,1,2,32]{3,2,1,0:T(2,128)} copy(f32[3,1,2,32]{3,2,1,0:T(2,128)S(1)} %copy-done) | data formatting | bytes 1536
Async XLA Ops:
  26.5 1.4 %copy-start = (f32[3,1,2,32]{3,2,1,0:T(2,128)S(1)}, f32[3,1,2,32]{3,2,1,0:T(2,128)}, u32[]{:S(2)}) copy-start(f32[3,1,2,32]{3,2,1,0:T(2,128)} %get-tuple-element.5) | copy-start | bytes 2308

commit v3 on v2

--- a/solution.py
+++ b/solution.py
@@ -151,7 +151,7 @@
 
 def kernel(
     nx, ny, pops_hbm, label_hbm, drive_hbm, table_hbm, forward_hbm, inverse_hbm, momentum_hbm, running_ref,
-    state, label, drive, table, forward, inverse_z, momentum, face_out, face_in, row_out, row_in, edge_out, edge_in,
+    state, stress, label, drive, table, forward, inverse_z, momentum, face_out, face_in, row_out, row_in, edge_out, edge_in,
     message, arrived, load_sem, const_sem, halo_send, halo_recv, slow_send, slow_recv, out_sem,
 ):
     width = label.shape[0]
@@ -172,28 +172,31 @@
     for copy in loads + constants:
         copy.start()
 
-    def device_at(far):
-        return (lax.rem(gx + far // ny, nx), lax.rem(gy + far % ny, ny))
+    def wrap(at, size):
+        return jnp.where(at >= size, at - size, at)
 
     def over_others(body):
-        if count <= 64:
-            for far in range(1, count):
-                body(far)
-        else:
-            def step(far, carry):
-                body(far)
-                return carry
-
-            lax.fori_loop(1, count, step, 0)
+        for dy in range(1, ny):
+            body(dy, (gx, wrap(gy + dy, ny)))
+
+        def step(dx, carry):
+            x = wrap(gx + dx, nx)
+            for dy in range(ny):
+                body(dx * ny + dy, (x, wrap(gy + dy, ny)))
+            return carry
+
+        lax.fori_loop(1, nx, step, 0)
 
     barrier = pltpu.get_barrier_semaphore()
-    over_others(lambda far: pl.semaphore_signal(barrier, inc=1, device_id=device_at(far), device_id_type=MESH))
+    over_others(lambda far, place: pl.semaphore_signal(barrier, inc=1, device_id=place, device_id_type=MESH))
+    for c in range(6):
+        stress[c] = jnp.zeros((8, NZ), jnp.float32)
 
     for copy in loads:
         copy.wait()
 
-    east, west = lax.rem(gx + 1, nx), lax.rem(gx + nx - 1, nx)
-    north, south = lax.rem(gy + 1, ny), lax.rem(gy + ny - 1, ny)
+    east, west = wrap(gx + 1, nx), wrap(gx + nx - 1, nx)
+    north, south = wrap(gy + 1, ny), wrap(gy + ny - 1, ny)
     side_x = {1: east, -1: west}
     side_y = {1: north, -1: south}
     slot = {1: 0, -1: 1}
@@ -212,12 +215,12 @@
         faces, rows = [], []
         for sign in (1, -1):
             s = slot[sign]
-            faces.append(remote(face_out.at[step, s], face_in.at[step, s], step, s, (side_x[sign], gy)))
+            faces.append(remote(face_out.at[step, s], face_in.at[step + 1, s], step, s, (side_x[sign], gy)))
         if ny == 2:
             for sign in (1, -1):
                 s = slot[sign]
-                faces.append(remote(edge_out.at[step, s], edge_in.at[step, s], step, 4 + s, (side_x[sign], north)))
-            rows.append(remote(row_out.at[step], row_in.at[step], step, 2, (gx, north)))
+                faces.append(remote(edge_out.at[step, s], edge_in.at[step + 1, s], step, 4 + s, (side_x[sign], north)))
+            rows.append(remote(row_out.at[step], row_in.at[step + 1], step, 2, (gx, north)))
         else:
             for sign in (1, -1):
                 s = slot[sign]
@@ -225,32 +228,28 @@
                     t = slot[turn]
                     faces.append(
                         remote(
-                            edge_out.at[step, t, s], edge_in.at[step, t, s], step, 4 + 2 * t + s,
+                            edge_out.at[step, t, s], edge_in.at[step + 1, t, s], step, 4 + 2 * t + s,
                             (side_x[turn], side_y[sign]),
                         )
                     )
-                rows.append(remote(row_out.at[step, s], row_in.at[step, s], step, 2 + s, (gx, side_y[sign])))
+                rows.append(remote(row_out.at[step, s], row_in.at[step + 1, s], step, 2 + s, (gx, side_y[sign])))
         return faces, rows
 
     row_id = lax.broadcasted_iota(jnp.int32, (8, NZ), 0)
-    first_row = row_id == 0
-    last_row = row_id == 7
-
-    def read(step, i, p):
+
+    def read(step, fresh, i, p):
         cx, cy, _ = VELOCITY[i]
-        if step == 0:
-            return state[0, i, p]
         outside = (cx == 1 and p == 0) or (cx == -1 and p == width - 1)
         if outside:
-            value = face_in[step - 1, slot[cx], CROSS[0, cx].index(i)]
+            value = face_in[step, slot[cx], CROSS[0, cx].index(i)]
         else:
-            value = state[step % 2, i, p]
+            value = state[step, i, p]
         if cy:
             if outside:
-                row = edge_in[step - 1, slot[cx], slot[cy]]
+                row = edge_in[step, slot[cx], slot[cy]]
             else:
-                row = row_in[step - 1, slot[cy], CROSS[1, cy].index(i) * width + p]
-            value = jnp.where(first_row if cy == 1 else last_row, jnp.broadcast_to(row, (8, NZ)), value)
+                row = row_in[step, slot[cy], CROSS[1, cy].index(i) * width + p]
+            value = jnp.where(row_id == fresh[cy], jnp.broadcast_to(row, (8, NZ)), value)
         return value
 
     def write(step, i, p, value):
@@ -266,73 +265,81 @@
             if cy:
                 edge_out[step, slot[cx], slot[cy]] = line
         else:
-            state[(step + 1) % 2, i, p + cx] = value
+            state[step + 1, i, p + cx] = value
             if cy:
                 row_out[step, slot[cy], CROSS[1, cy].index(i) * width + p + cx] = line
 
-    def send_copy(far):
+    def send_copy(far, place):
         return pltpu.make_async_remote_copy(
             src_ref=message.at[far],
             dst_ref=arrived.at[far],
             send_sem=slow_send,
             recv_sem=slow_recv,
-            device_id=device_at(far),
+            device_id=place,
             device_id_type=MESH,
         )
 
-    total = [None] * 6
-
-    def advance(step, p):
-        phase = math.cos(2.0 * math.pi * (step + 0.5) / STEPS)
-        f = [read(step, i, p) for i in range(19)]
-        rho, j = moments(f)
-        inverse = 1.0 / rho
-        kind = label[p]
-        solid = kind == 2
-        thin = jnp.where(solid, 0.0, inverse)
-        scaled = [one * thin for one in j]
-        for c, (a, b) in enumerate(PAIRS):
-            term = scaled[a] * j[b]
-            total[c] = term if total[c] is None else total[c] + term
-        second = kind == 1
-        omega = jnp.where(second, 1.1, 1.6)
-        strength = jnp.where(second, 0.6 * phase, phase)
-        push = [strength * drive[a, p] for a in range(3)]
-        post = collide(f, rho, j, inverse, 1.0 - omega, omega, push, solid)
-        for i in range(19):
-            write(step, i, p, post[i])
-
-    outer = [0, width - 1]
-    inner = list(range(1, width - 1))
-    started = []
-    for step in range(STEPS):
-        if step == 0:
-            for p in outer:
-                advance(step, p)
+    def advance(step, planes):
+        quarter = math.cos(math.pi / 4.0)
+        phase = jnp.where((step == 0) | (step == STEPS - 1), quarter, -quarter)
+        fresh = {1: jnp.where(step > 0, 0, -1), -1: jnp.where(step > 0, 7, -1)}
+        total = [None] * 6
+        for p in planes:
+            f = [read(step, fresh, i, p) for i in range(19)]
+            rho, j = moments(f)
+            inverse = 1.0 / rho
+            kind = label[p]
+            solid = kind == 2
+            thin = jnp.where(solid, 0.0, inverse)
+            scaled = [one * thin for one in j]
+            for c, (a, b) in enumerate(PAIRS):
+                term = scaled[a] * j[b]
+                total[c] = term if total[c] is None else total[c] + term
+            second = kind == 1
+            omega = jnp.where(second, 1.1, 1.6)
+            strength = jnp.where(second, 0.6 * phase, phase)
+            push = [strength * drive[a, p] for a in range(3)]
+            post = collide(f, rho, j, inverse, 1.0 - omega, omega, push, solid)
+            for i in range(19):
+                write(step, i, p, post[i])
+        for c in range(6):
+            stress[c] += total[c]
+
+    for sign in (1, -1):
+        for k, i in enumerate(CROSS[0, sign]):
+            face_in[0, slot[sign], k] = state[0, i, 0 if sign == 1 else width - 1]
+
+    def cycle_step(step, carry):
+        @pl.when(step > 0)
+        def _():
+            for copy in halo(step - 1)[1]:
+                copy.wait_recv()
+
+        advance(step, range(1, width - 1))
+
+        @pl.when(step > 0)
+        def _():
+            for copy in halo(step - 1)[0]:
+                copy.wait_recv()
+
+        advance(step, [0, width - 1])
+
+        @pl.when(step == 0)
+        def _():
             pl.semaphore_wait(barrier, count - 1)
-        else:
-            for copy in rows:
-                copy.wait_recv()
-            for p in inner:
-                advance(step, p)
-            for copy in faces:
-                copy.wait_recv()
-            for p in outer:
-                advance(step, p)
+
         faces, rows = halo(step)
-        started += faces + rows
-        for copy in faces:
+        for copy in faces + rows:
             copy.start()
-        if step == 0:
-            for p in inner:
-                advance(step, p)
-        for copy in rows:
-            copy.start()
+        return carry
+
+    lax.fori_loop(0, STEPS, cycle_step, 0)
+    faces, rows = halo(STEPS - 1)
 
     for copy in constants:
         copy.wait()
-    plain = dot(jnp.concatenate(total[:EVEN], axis=0), forward[:, :NZ])
-    turned = dot(jnp.concatenate(total[EVEN:], axis=0), forward[:, NZ:])
+    plain = dot(stress[:EVEN].reshape(8 * EVEN, NZ), forward[:, :NZ])
+    turned = dot(stress[EVEN:].reshape(8 * (6 - EVEN), NZ), forward[:, NZ:])
     lines = []
     for c in range(6):
         tile = plain[8 * c : 8 * c + 8] if c < EVEN else turned[8 * (c - EVEN) : 8 * (c - EVEN) + 8]
@@ -357,12 +364,12 @@
             return carry
 
         lax.fori_loop(0, count // 4, each, 0)
-    over_others(lambda far: send_copy(far).start())
+    over_others(lambda far, place: send_copy(far, place).start())
 
     for copy in faces + rows:
         copy.wait_recv()
     for p in range(width):
-        f = [None] + [read(STEPS, i, p) for i in range(1, 19)]
+        f = [None] + [read(STEPS, {1: 0, -1: 7}, i, p) for i in range(1, 19)]
         for axis in range(3):
             value = None
             for i in range(1, 19):
@@ -372,8 +379,9 @@
             momentum[axis, p] = value
     out_copy = pltpu.make_async_copy(momentum, momentum_hbm, out_sem)
     out_copy.start()
-    for copy in started:
-        copy.wait_send()
+    for step in range(STEPS):
+        for copy in halo(step)[0] + halo(step)[1]:
+            copy.wait_send()
 
     rest = pl.ds(1, count - 1)
     pltpu.make_async_copy(message.at[rest], arrived.at[rest], slow_recv).wait()
@@ -413,7 +421,8 @@
         in_specs=[anywhere] * 6,
         out_specs=(anywhere, pl.BlockSpec(memory_space=pltpu.VMEM)),
         scratch_shapes=[
-            pltpu.VMEM((2, 19, width, height, NZ), f32),
+            pltpu.VMEM((STEPS + 1, 19, width, height, NZ), f32),
+            pltpu.VMEM((6, height, NZ), f32),
             pltpu.VMEM((width, height, NZ), jnp.int32),
             pltpu.VMEM((3, width, height, NZ), f32),
             pltpu.VMEM(send.shape, f32),
@@ -421,11 +430,11 @@
             pltpu.VMEM(inverse.shape, f32),
             pltpu.VMEM((3, width, height, NZ), f32),
             pltpu.VMEM((STEPS, 2, 5, height, NZ), f32),
-            pltpu.VMEM((STEPS, 2, 5, height, NZ), f32),
+            pltpu.VMEM((STEPS + 1, 2, 5, height, NZ), f32),
             pltpu.VMEM((STEPS, 2, 5 * width, 1, NZ), f32),
-            pltpu.VMEM((STEPS, 2, 5 * width, 1, NZ), f32),
+            pltpu.VMEM((STEPS + 1, 2, 5 * width, 1, NZ), f32),
             pltpu.VMEM((STEPS, 2, 2, 1, NZ), f32),
-            pltpu.VMEM((STEPS, 2, 2, 1, NZ), f32),
+            pltpu.VMEM((STEPS + 1, 2, 2, 1, NZ), f32),
             pltpu.VMEM((count, 2, NZ), f32),
             pltpu.VMEM((count, 2, NZ), f32),
             pltpu.SemaphoreType.DMA((3,)),

time: 28.7 us -> 28.7 us (level)
  no operation moved by 1% of the time
where the time goes in v3:
time: 28.7 us; the launch traced here: 28.6 us
  Pallas kernels  25.9 us (90%)
  local copies, waits for them, and re-layouts  2 us (7%)
  between operations  0.65 us (2%)
    pallas_call x1, Pallas kernels, local(): pl.pallas_call(functools.partial(kernel, nx, ny), out_shape=(jax.ShapeDty...  25.9 us
    unnamed x4, local copies, waits for them, and re-layouts  2 us

profile of v3, /device:TPU:0, one launch (start us, length us, event | category | flops | bytes accessed | tf_op | source)
XLA Modules:
  0.0 28.6 jit_solution(1203390462284445020)
XLA Ops:
  0.6 25.9 %cycle.1 = (f32[3,4,8,128]{3,2,1,0:T(8,128)}, f32[3,1,2,32]{3,2,1,0:T(2,128)}) custom-call(f32[19,4,8,128]{3,2,1,0:T(8,128)} %pops_hbm.1, s32[4,8,128]{2,1,0:T(8,128)} %label_hbm.1, f32[3,4,8,128]{3,2,1,0:T(8,128)} %drive_hbm.1, f32[8,12,8,128]{3,2,1,0:T(8,128)} %constant.6.clone.table_hbm, f32[128,256]{1,0:T(8,128)} %constant.7.clone.forward_hbm, ...), custom_call_target="tpu_custom_call" | custom-call | tf_op jit(solution)/shard_map/cycle/pallas_call | solution.py:415
  26.5 0.0 copy-start
  26.5 1.4 %copy.10 = f32[3,4,8,128]{3,2,1,0:T(8,128)} copy(f32[3,4,8,128]{3,2,1,0:T(8,128)} %get-tuple-element.4) | data formatting | bytes 98304
  28.0 0.0 copy-done
  28.0 0.6 %copy.11 = f32[3,1,2,32]{3,2,1,0:T(2,128)} copy(f32[3,1,2,32]{3,2,1,0:T(2,128)S(1)} %copy-done) | data formatting | bytes 1536
Async XLA Ops:
  26.5 1.4 %copy-start = (f32[3,1,2,32]{3,2,1,0:T(2,128)S(1)}, f32[3,1,2,32]{3,2,1,0:T(2,128)}, u32[]{:S(2)}) copy-start(f32[3,1,2,32]{3,2,1,0:T(2,128)} %get-tuple-element.5) | copy-start | bytes 2308

commit v4 on v3

--- a/solution.py
+++ b/solution.py
@@ -150,9 +150,9 @@
 
 
 def kernel(
-    nx, ny, pops_hbm, label_hbm, drive_hbm, table_hbm, forward_hbm, inverse_hbm, momentum_hbm, running_ref,
-    state, stress, label, drive, table, forward, inverse_z, momentum, face_out, face_in, row_out, row_in, edge_out, edge_in,
-    message, arrived, load_sem, const_sem, halo_send, halo_recv, slow_send, slow_recv, out_sem,
+    nx, ny, pops_hbm, label_hbm, drive_hbm, table_hbm, forward_hbm, inverse_hbm, momentum, running_ref,
+    state, stress, label, drive, table, forward, inverse_z, face_out, face_in, row_out, row_in, edge_out, edge_in,
+    message, arrived, load_sem, const_sem, halo_send, halo_recv, slow_send, slow_recv,
 ):
     width = label.shape[0]
     gx = lax.axis_index("gx")
@@ -377,8 +377,6 @@
                 if c:
                     value = c * f[i] if value is None else value + f[i] if c > 0 else value - f[i]
             momentum[axis, p] = value
-    out_copy = pltpu.make_async_copy(momentum, momentum_hbm, out_sem)
-    out_copy.start()
     for step in range(STEPS):
         for copy in halo(step)[0] + halo(step)[1]:
             copy.wait_send()
@@ -403,7 +401,6 @@
     for a in range(3):
         running_ref[a, 0] = result[2 * a : 2 * a + 2, :slow_z]
     pltpu.make_async_copy(arrived.at[rest], message.at[rest], slow_send).wait()
-    out_copy.wait()
 
 
 def local(nx, ny, constants, pops, label, drive):
@@ -415,11 +412,11 @@
     return pl.pallas_call(
         functools.partial(kernel, nx, ny),
         out_shape=(
-            jax.ShapeDtypeStruct((3, width, height, NZ), f32),
-            jax.ShapeDtypeStruct((3, width // CUT, height // CUT, NZ // CUT), f32),
+            pltpu.VMEM((3, width, height, NZ), f32),
+            pltpu.VMEM((3, width // CUT, height // CUT, NZ // CUT), f32),
         ),
         in_specs=[anywhere] * 6,
-        out_specs=(anywhere, pl.BlockSpec(memory_space=pltpu.VMEM)),
+        out_specs=(pl.BlockSpec(memory_space=pltpu.VMEM),) * 2,
         scratch_shapes=[
             pltpu.VMEM((STEPS + 1, 19, width, height, NZ), f32),
             pltpu.VMEM((6, height, NZ), f32),
@@ -428,7 +425,6 @@
             pltpu.VMEM(send.shape, f32),
             pltpu.VMEM(forward.shape, f32),
             pltpu.VMEM(inverse.shape, f32),
-            pltpu.VMEM((3, width, height, NZ), f32),
             pltpu.VMEM((STEPS, 2, 5, height, NZ), f32),
             pltpu.VMEM((STEPS + 1, 2, 5, height, NZ), f32),
             pltpu.VMEM((STEPS, 2, 5 * width, 1, NZ), f32),
@@ -443,7 +439,6 @@
             pltpu.SemaphoreType.DMA((STEPS, MESSAGES)),
             pltpu.SemaphoreType.DMA,
             pltpu.SemaphoreType.DMA,
-            pltpu.SemaphoreType.DMA,
         ],
         compiler_params=pltpu.CompilerParams(
             collective_id=0, has_side_effects=True, vmem_limit_bytes=60 * 1024 * 1024

time: 28.7 us -> 27 us (0.941)
  Pallas kernels: 25.9 us -> 25 us
  local copies, waits for them, and re-layouts: 2 us -> 1.2 us
    pallas_call x1, Pallas kernels: 25.9 us -> 25 us  [local(): pl.pallas_call(functools.partial(kernel, nx, ny), out_shape=(pltpu.VMEM((...]
    unnamed x4 -> x2, local copies, waits for them, and re-layouts: 2 us -> 1.2 us
where the time goes in v4:
time: 27 us; the launch traced here: 26.9 us
  Pallas kernels  25 us (93%)
  local copies, waits for them, and re-layouts  1.2 us (4%)
  between operations  0.64 us (2%)
    pallas_call x1, Pallas kernels, local(): pl.pallas_call(functools.partial(kernel, nx, ny), out_shape=(pltpu.VMEM((...  25 us
    unnamed x2, local copies, waits for them, and re-layouts  1.2 us

profile of v4, /device:TPU:0, one launch (start us, length us, event | category | flops | bytes accessed | tf_op | source)
XLA Modules:
  0.0 26.9 jit_solution(18400621902126104440)
XLA Ops:
  0.6 25.0 %cycle.1 = (f32[3,4,8,128]{3,2,1,0:T(8,128)S(1)}, f32[3,1,2,32]{3,2,1,0:T(2,128)S(1)}) custom-call(f32[19,4,8,128]{3,2,1,0:T(8,128)} %pops_hbm.1, s32[4,8,128]{2,1,0:T(8,128)} %label_hbm.1, f32[3,4,8,128]{3,2,1,0:T(8,128)} %drive_hbm.1, f32[8,12,8,128]{3,2,1,0:T(8,128)} %constant.6.clone.table_hbm, f32[128,256]{1,0:T(8,128)} %constant.7.clone.forward_hbm, ...), custom_call_target="tpu_custom_call" | custom-call | tf_op jit(solution)/shard_map/cycle/pallas_call | solution.py:412
  25.7 0.6 %copy.10 = f32[3,4,8,128]{3,2,1,0:T(8,128)} copy(f32[3,4,8,128]{3,2,1,0:T(8,128)S(1)} %get-tuple-element.2) | data formatting | bytes 98304
  26.3 0.6 %copy.11 = f32[3,1,2,32]{3,2,1,0:T(2,128)} copy(f32[3,1,2,32]{3,2,1,0:T(2,128)S(1)} %get-tuple-element.3) | data formatting | bytes 1536

commit v5 on v4

--- a/solution.py
+++ b/solution.py
@@ -68,6 +68,13 @@
     return out
 
 
+def split(table):
+    table = table.astype(np.float32)
+    high = table.astype(jnp.bfloat16)
+    low = (table - high.astype(np.float32)).astype(jnp.bfloat16)
+    return np.concatenate([high, low], axis=1)
+
+
 def tables(nx, ny):
     slow = NZ // CUT
     half = slow // 2
@@ -96,19 +103,21 @@
     plain = np.concatenate([cosine, -sine[:, 1:half]], axis=1)
     turned = np.concatenate([cosine[:, :1], sine[:, 1:half], cosine[:, half:], cosine[:, 1:half]], axis=1)
     scale = 1.0 / (STEPS * CUT**3)
-    forward = np.concatenate([np.tile(plain, (CUT, 1, 4)).reshape(CUT, slow, NZ).transpose(1, 0, 2).reshape(NZ, NZ),
-                              np.tile(turned, (CUT, 1, 4)).reshape(CUT, slow, NZ).transpose(1, 0, 2).reshape(NZ, NZ)], axis=1)
-    forward = forward * scale
+    forward = np.stack([split(np.repeat(np.tile(one, (1, 4)), CUT, axis=0) * scale) for one in (plain, turned)])
     edge = [cosine[:, :1], cosine[:, half:]]
     back = np.concatenate([edge[0], 2 * cosine[:, 1:half], edge[1], -2 * sine[:, 1:half]], axis=1).T / slow
     back_turned = np.concatenate([edge[0], -2 * sine[:, 1:half], edge[1], -2 * cosine[:, 1:half]], axis=1).T / slow
     inverse = np.concatenate([back, back, back_turned, back_turned], axis=0)
-    inverse = np.concatenate([inverse, np.zeros((NZ, NZ - slow))], axis=1)
-    return send.astype(np.float32), forward.astype(np.float32), inverse.astype(np.float32)
+    inverse = split(np.concatenate([inverse, np.zeros((NZ, NZ - slow))], axis=1))
+    return send.astype(np.float32), forward, inverse
 
 
 def dot(left, right):
-    return jnp.dot(left, right, precision=lax.Precision.HIGHEST, preferred_element_type=jnp.float32)
+    rows = left.shape[0]
+    high = left.astype(jnp.bfloat16).astype(jnp.float32)
+    parts = jnp.concatenate([high, left - high], axis=0).astype(jnp.bfloat16)
+    both = jnp.dot(parts, right, preferred_element_type=jnp.float32)
+    return both[:rows, :NZ] + (both[:rows, NZ:] + both[rows:, :NZ])
 
 
 def moments(f):
@@ -169,9 +178,6 @@
         pltpu.make_async_copy(forward_hbm, forward, const_sem.at[1]),
         pltpu.make_async_copy(inverse_hbm, inverse_z, const_sem.at[2]),
     ]
-    for copy in loads + constants:
-        copy.start()
-
     def wrap(at, size):
         return jnp.where(at >= size, at - size, at)
 
@@ -189,6 +195,8 @@
 
     barrier = pltpu.get_barrier_semaphore()
     over_others(lambda far, place: pl.semaphore_signal(barrier, inc=1, device_id=place, device_id_type=MESH))
+    for copy in loads + constants:
+        copy.start()
     for c in range(6):
         stress[c] = jnp.zeros((8, NZ), jnp.float32)
 
@@ -212,27 +220,26 @@
         )
 
     def halo(step):
-        faces, rows = [], []
+        faces, rows = {}, []
         for sign in (1, -1):
             s = slot[sign]
-            faces.append(remote(face_out.at[step, s], face_in.at[step + 1, s], step, s, (side_x[sign], gy)))
+            faces[sign] = [remote(face_out.at[step, s], face_in.at[step + 1, s], step, s, (side_x[sign], gy))]
+            if ny == 2:
+                faces[sign].append(
+                    remote(edge_out.at[step, s], edge_in.at[step + 1, s], step, 4 + s, (side_x[sign], north))
+                )
+                continue
+            for turn in (1, -1):
+                t = slot[turn]
+                faces[sign].append(
+                    remote(
+                        edge_out.at[step, s, t], edge_in.at[step + 1, s, t], step, 4 + 2 * s + t,
+                        (side_x[sign], side_y[turn]),
+                    )
+                )
+            rows.append(remote(row_out.at[step, s], row_in.at[step + 1, s], step, 2 + s, (gx, side_y[sign])))
         if ny == 2:
-            for sign in (1, -1):
-                s = slot[sign]
-                faces.append(remote(edge_out.at[step, s], edge_in.at[step + 1, s], step, 4 + s, (side_x[sign], north)))
             rows.append(remote(row_out.at[step], row_in.at[step + 1], step, 2, (gx, north)))
-        else:
-            for sign in (1, -1):
-                s = slot[sign]
-                for turn in (1, -1):
-                    t = slot[turn]
-                    faces.append(
-                        remote(
-                            edge_out.at[step, t, s], edge_in.at[step + 1, t, s], step, 4 + 2 * t + s,
-                            (side_x[turn], side_y[sign]),
-                        )
-                    )
-                rows.append(remote(row_out.at[step, s], row_in.at[step + 1, s], step, 2 + s, (gx, side_y[sign])))
         return faces, rows
 
     row_id = lax.broadcasted_iota(jnp.int32, (8, NZ), 0)
@@ -279,67 +286,105 @@
             device_id_type=MESH,
         )
 
-    def advance(step, planes):
+    def phase_of(step):
         quarter = math.cos(math.pi / 4.0)
-        phase = jnp.where((step == 0) | (step == STEPS - 1), quarter, -quarter)
+        return jnp.where((step == 0) | (step == STEPS - 1), quarter, -quarter)
+
+    def measure(step, planes):
         fresh = {1: jnp.where(step > 0, 0, -1), -1: jnp.where(step > 0, 7, -1)}
         total = [None] * 6
+        held = []
         for p in planes:
             f = [read(step, fresh, i, p) for i in range(19)]
             rho, j = moments(f)
             inverse = 1.0 / rho
-            kind = label[p]
-            solid = kind == 2
-            thin = jnp.where(solid, 0.0, inverse)
+            thin = jnp.where(label[p] == 2, 0.0, inverse)
             scaled = [one * thin for one in j]
             for c, (a, b) in enumerate(PAIRS):
                 term = scaled[a] * j[b]
                 total[c] = term if total[c] is None else total[c] + term
-            second = kind == 1
+            held.append((p, f, rho, j, inverse))
+        for c in range(6):
+            stress[c] += total[c]
+        return held
+
+    def finish(step, held):
+        phase = phase_of(step)
+        for p, f, rho, j, inverse in held:
+            second = label[p] == 1
             omega = jnp.where(second, 1.1, 1.6)
             strength = jnp.where(second, 0.6 * phase, phase)
             push = [strength * drive[a, p] for a in range(3)]
-            post = collide(f, rho, j, inverse, 1.0 - omega, omega, push, solid)
+            post = collide(f, rho, j, inverse, 1.0 - omega, omega, push, label[p] == 2)
             for i in range(19):
                 write(step, i, p, post[i])
-        for c in range(6):
-            stress[c] += total[c]
+
+    def advance(step, planes):
+        for p in planes:
+            finish(step, measure(step, [p]))
 
     for sign in (1, -1):
         for k, i in enumerate(CROSS[0, sign]):
             face_in[0, slot[sign], k] = state[0, i, 0 if sign == 1 else width - 1]
 
+    inner = list(range(1, width - 1))
+    far_side = gx == nx - 1
+
+    def start_step(step):
+        for copy in halo(step - 1)[1]:
+            copy.wait_recv()
+        advance(step, inner)
+
+    def side(step, sign):
+        for copy in halo(step - 1)[0][-sign]:
+            copy.wait_recv()
+        advance(step, [width - 1 if sign == 1 else 0])
+        for copy in halo(step)[0][sign]:
+            copy.start()
+
+    advance(0, [0, width - 1])
+    pl.semaphore_wait(barrier, count - 1)
+    faces, rows = halo(0)
+    for copy in faces[1] + faces[-1]:
+        copy.start()
+    advance(0, inner)
+    for copy in rows:
+        copy.start()
+
     def cycle_step(step, carry):
-        @pl.when(step > 0)
+        start_step(step)
+
+        @pl.when(far_side)
         def _():
-            for copy in halo(step - 1)[1]:
-                copy.wait_recv()
-
-        advance(step, range(1, width - 1))
-
-        @pl.when(step > 0)
+            side(step, -1)
+            side(step, 1)
+
+        @pl.when(jnp.logical_not(far_side))
         def _():
-            for copy in halo(step - 1)[0]:
-                copy.wait_recv()
-
-        advance(step, [0, width - 1])
-
-        @pl.when(step == 0)
-        def _():
-            pl.semaphore_wait(barrier, count - 1)
-
-        faces, rows = halo(step)
-        for copy in faces + rows:
+            side(step, 1)
+            side(step, -1)
+
+        for copy in halo(step)[1]:
             copy.start()
         return carry
 
-    lax.fori_loop(0, STEPS, cycle_step, 0)
-    faces, rows = halo(STEPS - 1)
-
+    lax.fori_loop(1, STEPS - 1, cycle_step, 0)
+    step = STEPS - 1
+    start_step(step)
     for copy in constants:
         copy.wait()
-    plain = dot(stress[:EVEN].reshape(8 * EVEN, NZ), forward[:, :NZ])
-    turned = dot(stress[EVEN:].reshape(8 * (6 - EVEN), NZ), forward[:, NZ:])
+    for sign in (1, -1):
+        for copy in halo(step - 1)[0][sign]:
+            copy.wait_recv()
+    held = measure(step, [0, width - 1])
+    plain = dot(stress[:EVEN].reshape(8 * EVEN, NZ), forward[0])
+    turned = dot(stress[EVEN:].reshape(8 * (6 - EVEN), NZ), forward[1])
+    finish(step, held)
+    faces, rows = halo(step)
+    last = faces[1] + faces[-1] + rows
+    for copy in last:
+        copy.start()
+
     lines = []
     for c in range(6):
         tile = plain[8 * c : 8 * c + 8] if c < EVEN else turned[8 * (c - EVEN) : 8 * (c - EVEN) + 8]
@@ -366,7 +411,7 @@
         lax.fori_loop(0, count // 4, each, 0)
     over_others(lambda far, place: send_copy(far, place).start())
 
-    for copy in faces + rows:
+    for copy in last:
         copy.wait_recv()
     for p in range(width):
         f = [None] + [read(STEPS, {1: 0, -1: 7}, i, p) for i in range(1, 19)]
@@ -378,7 +423,8 @@
                     value = c * f[i] if value is None else value + f[i] if c > 0 else value - f[i]
             momentum[axis, p] = value
     for step in range(STEPS):
-        for copy in halo(step)[0] + halo(step)[1]:
+        faces, rows = halo(step)
+        for copy in faces[1] + faces[-1] + rows:
             copy.wait_send()
 
     rest = pl.ds(1, count - 1)
@@ -423,8 +469,8 @@
             pltpu.VMEM((width, height, NZ), jnp.int32),
             pltpu.VMEM((3, width, height, NZ), f32),
             pltpu.VMEM(send.shape, f32),
-            pltpu.VMEM(forward.shape, f32),
-            pltpu.VMEM(inverse.shape, f32),
+            pltpu.VMEM(forward.shape, forward.dtype),
+            pltpu.VMEM(inverse.shape, inverse.dtype),
             pltpu.VMEM((STEPS, 2, 5, height, NZ), f32),
             pltpu.VMEM((STEPS + 1, 2, 5, height, NZ), f32),
             pltpu.VMEM((STEPS, 2, 5 * width, 1, NZ), f32),

time: 27 us -> 26.9 us (level)
  no operation moved by 1% of the time
where the time goes in v5:
time: 26.9 us; the launch traced here: 26.8 us
  Pallas kernels  24.9 us (93%)
  local copies, waits for them, and re-layouts  1.2 us (4%)
  between operations  0.64 us (2%)
    pallas_call x1, Pallas kernels, local(): pl.pallas_call(functools.partial(kernel, nx, ny), out_shape=(pltpu.VMEM((...  24.9 us
    unnamed x2, local copies, waits for them, and re-layouts  1.2 us

profile of v5, /device:TPU:0, one launch (start us, length us, event | category | flops | bytes accessed | tf_op | source)
XLA Modules:
  0.0 26.8 jit_solution(6730847632697321505)
XLA Ops:
  0.6 24.9 %cycle.1 = (f32[3,4,8,128]{3,2,1,0:T(8,128)S(1)}, f32[3,1,2,32]{3,2,1,0:T(2,128)S(1)}) custom-call(f32[19,4,8,128]{3,2,1,0:T(8,128)} %pops_hbm.1, s32[4,8,128]{2,1,0:T(8,128)} %label_hbm.1, f32[3,4,8,128]{3,2,1,0:T(8,128)} %drive_hbm.1, f32[8,12,8,128]{3,2,1,0:T(8,128)} %constant.6.clone.table_hbm, bf16[2,128,256]{2,1,0:T(8,128)(2,1)} %constant.7.clone.forward_hbm, ...), custom_call_target="tpu_custom_call" | custom-call | tf_op jit(solution)/shard_map/cycle/pallas_call | solution.py:458
  25.6 0.6 %copy.10 = f32[3,4,8,128]{3,2,1,0:T(8,128)} copy(f32[3,4,8,128]{3,2,1,0:T(8,128)S(1)} %get-tuple-element.2) | data formatting | bytes 98304
  26.2 0.6 %copy.11 = f32[3,1,2,32]{3,2,1,0:T(2,128)} copy(f32[3,1,2,32]{3,2,1,0:T(2,128)S(1)} %get-tuple-element.3) | data formatting | bytes 1536

commit v6 on v5

--- a/solution.py
+++ b/solution.py
@@ -41,6 +41,7 @@
 CROSS = {
     (axis, sign): [i for i in range(19) if VELOCITY[i][axis] == sign] for axis in (0, 1) for sign in (1, -1)
 }
+GROUP = 4
 MESSAGES = 8
 
 
@@ -80,23 +81,23 @@
     half = slow // 2
     green = response(nx, 2 * ny, slow)
     count = nx * ny
-    send = np.zeros((count, 12, 2, 4, slow))
+    send = np.zeros((GROUP, count, 12, 2, 4, slow))
     place = {(0, 0): (0, 0), (0, 1): (0, 1), (2, 0): (0, 2), (2, 1): (0, 3), (1, 0): (1, 0), (1, 1): (1, 1)}
-    far_x = np.arange(count) // ny
-    far_y = np.arange(count) % ny
+    far_x = np.arange(count) // ny - np.arange(GROUP)[:, None]
+    far_y = np.arange(count) % ny + np.zeros((GROUP, 1), np.int64)
     for c in range(6):
         for half_y in range(2):
             for (a, to_y), (row, block) in place.items():
-                g = green[a, c][far_x, (2 * far_y + to_y - half_y) % (2 * ny)]
-                inside = g[:, 1:half]
+                g = green[a, c][far_x % nx, (2 * far_y + to_y - half_y) % (2 * ny)]
+                inside = g[..., 1:half]
                 if a < 2:
                     inside = inside.real if c < EVEN else inside.imag
                 else:
                     inside = inside.imag if c < EVEN else -inside.real
-                send[:, 2 * c + half_y, row, block, : half + 1] = g.real
-                send[:, 2 * c + half_y, row, block, 1:half] = inside
-                send[:, 2 * c + half_y, row, block, half + 1 :] = inside
-    send = send.reshape(count // 4, 4, 12, 2, NZ).transpose(0, 2, 1, 3, 4).reshape(count // 4, 12, 8, NZ)
+                send[:, :, 2 * c + half_y, row, block, : half + 1] = g.real
+                send[:, :, 2 * c + half_y, row, block, 1:half] = inside
+                send[:, :, 2 * c + half_y, row, block, half + 1 :] = inside
+    send = send.reshape(GROUP, count // 4, 4, 12, 2, NZ).transpose(0, 1, 3, 2, 4, 5).reshape(GROUP, count // 4, 12, 8, NZ)
     place_z = np.arange(slow)
     angle = 2.0 * np.pi * place_z[:, None] * np.arange(half + 1)[None, :] / slow
     cosine, sine = np.cos(angle), np.sin(angle)
@@ -161,7 +162,7 @@
 def kernel(
     nx, ny, pops_hbm, label_hbm, drive_hbm, table_hbm, forward_hbm, inverse_hbm, momentum, running_ref,
     state, stress, label, drive, table, forward, inverse_z, face_out, face_in, row_out, row_in, edge_out, edge_in,
-    message, arrived, load_sem, const_sem, halo_send, halo_recv, slow_send, slow_recv,
+    message, arrived, summed, final, load_sem, const_sem, halo_send, halo_recv, slow_send, slow_recv,
 ):
     width = label.shape[0]
     gx = lax.axis_index("gx")
@@ -174,27 +175,32 @@
         pltpu.make_async_copy(drive_hbm, drive, load_sem.at[2]),
     ]
     constants = [
-        pltpu.make_async_copy(table_hbm, table, const_sem.at[0]),
+        pltpu.make_async_copy(table_hbm.at[lax.rem(gx, GROUP)], table, const_sem.at[0]),
         pltpu.make_async_copy(forward_hbm, forward, const_sem.at[1]),
         pltpu.make_async_copy(inverse_hbm, inverse_z, const_sem.at[2]),
     ]
     def wrap(at, size):
         return jnp.where(at >= size, at - size, at)
 
-    def over_others(body):
-        for dy in range(1, ny):
-            body(dy, (gx, wrap(gy + dy, ny)))
-
-        def step(dx, carry):
-            x = wrap(gx + dx, nx)
-            for dy in range(ny):
-                body(dx * ny + dy, (x, wrap(gy + dy, ny)))
-            return carry
-
-        lax.fori_loop(1, nx, step, 0)
-
+    east, west = wrap(gx + 1, nx), wrap(gx + nx - 1, nx)
+    north, south = wrap(gy + 1, ny), wrap(gy + ny - 1, ny)
+    side_x = {1: east, -1: west}
+    side_y = {1: north, -1: south}
+    groups = nx // GROUP
+    share = GROUP * ny
+    place = lax.rem(gx, GROUP)
+    base = gx - place
+    edges = [north] if ny == 2 else [north, south]
+    friends = [(x, y) for x in (east, west) for y in [gy] + edges] + [(gx, y) for y in edges]
+    afar = [(wrap(gx + GROUP * k, nx), gy) for k in range(1, groups)]
+    near = []
+    for k in range(1, share):
+        at = wrap(place + k // ny, GROUP)
+        near.append((at * ny + k % ny, (base + at, wrap(gy + k % ny, ny))))
+    greeted = friends + afar + [spot for _, spot in near]
     barrier = pltpu.get_barrier_semaphore()
-    over_others(lambda far, place: pl.semaphore_signal(barrier, inc=1, device_id=place, device_id_type=MESH))
+    for spot in greeted:
+        pl.semaphore_signal(barrier, inc=1, device_id=spot, device_id_type=MESH)
     for copy in loads + constants:
         copy.start()
     for c in range(6):
@@ -203,10 +209,6 @@
     for copy in loads:
         copy.wait()
 
-    east, west = wrap(gx + 1, nx), wrap(gx + nx - 1, nx)
-    north, south = wrap(gy + 1, ny), wrap(gy + ny - 1, ny)
-    side_x = {1: east, -1: west}
-    side_y = {1: north, -1: south}
     slot = {1: 0, -1: 1}
 
     def remote(src, dst, step, number, place):
@@ -276,13 +278,13 @@
             if cy:
                 row_out[step, slot[cy], CROSS[1, cy].index(i) * width + p + cx] = line
 
-    def send_copy(far, place):
+    def slow_copy(src, dst, stage, spot):
         return pltpu.make_async_remote_copy(
-            src_ref=message.at[far],
-            dst_ref=arrived.at[far],
-            send_sem=slow_send,
-            recv_sem=slow_recv,
-            device_id=place,
+            src_ref=src,
+            dst_ref=dst,
+            send_sem=slow_send.at[stage],
+            recv_sem=slow_recv.at[stage],
+            device_id=spot,
             device_id_type=MESH,
         )
 
@@ -343,7 +345,7 @@
             copy.start()
 
     advance(0, [0, width - 1])
-    pl.semaphore_wait(barrier, count - 1)
+    pl.semaphore_wait(barrier, len(greeted))
     faces, rows = halo(0)
     for copy in faces[1] + faces[-1]:
         copy.start()
@@ -393,23 +395,35 @@
         lines.append(jnp.broadcast_to(tile[0:1], (8, NZ)))
         lines.append(jnp.broadcast_to(tile[4:5], (8, NZ)))
 
-    def group(g):
-        value = lines[0] * table[g, 0]
-        for k in range(1, 12):
-            value = value + lines[k] * table[g, k]
-        for k in range(4):
-            message[4 * g + k] = value[2 * k : 2 * k + 2]
+    def shares(k):
+        for g in range(share // 4):
+            row = k * (share // 4) + g
+            value = lines[0] * table[row, 0]
+            for n in range(1, 12):
+                value = value + lines[n] * table[row, n]
+            for n in range(4):
+                message[k, 4 * g + n] = value[2 * n : 2 * n + 2]
 
     if count <= 64:
-        for g in range(count // 4):
-            group(g)
+        for k in range(groups):
+            shares(k)
     else:
-        def each(g, carry):
-            group(g)
+        def each(k, carry):
+            shares(k)
             return carry
 
-        lax.fori_loop(0, count // 4, each, 0)
-    over_others(lambda far, place: send_copy(far, place).start())
+        lax.fori_loop(0, groups, each, 0)
+    for k in range(1, groups):
+        slow_copy(message.at[k], arrived.at[k], 0, afar[k - 1]).start()
+    others = pl.ds(1, groups - 1)
+    pltpu.make_async_copy(message.at[others], arrived.at[others], slow_recv.at[0]).wait()
+    value = message[0]
+    for k in range(1, groups):
+        value = value + arrived[k]
+    summed[...] = value
+    for k in range(1, share):
+        target, spot = near[k - 1]
+        slow_copy(summed.at[target], final.at[k], 1, spot).start()
 
     for copy in last:
         copy.wait_recv()
@@ -427,14 +441,11 @@
         for copy in faces[1] + faces[-1] + rows:
             copy.wait_send()
 
-    rest = pl.ds(1, count - 1)
-    pltpu.make_async_copy(message.at[rest], arrived.at[rest], slow_recv).wait()
-    spectrum = message[0]
-    if count <= 64:
-        for far in range(1, count):
-            spectrum = spectrum + arrived[far]
-    else:
-        spectrum = lax.fori_loop(1, count, lambda far, value: value + arrived[far], spectrum)
+    rest = pl.ds(1, share - 1)
+    pltpu.make_async_copy(summed.at[rest], final.at[rest], slow_recv.at[1]).wait()
+    spectrum = summed[place * ny]
+    for k in range(1, share):
+        spectrum = spectrum + final[k]
     upper = jnp.broadcast_to(spectrum[0:1], (8, NZ))
     lower = jnp.broadcast_to(spectrum[1:2], (8, NZ))
     lane = lax.broadcasted_iota(jnp.int32, (8, NZ), 1)
@@ -446,12 +457,12 @@
     result = dot(spread, inverse_z[...])
     for a in range(3):
         running_ref[a, 0] = result[2 * a : 2 * a + 2, :slow_z]
-    pltpu.make_async_copy(arrived.at[rest], message.at[rest], slow_send).wait()
+    pltpu.make_async_copy(arrived.at[others], message.at[others], slow_send.at[0]).wait()
+    pltpu.make_async_copy(final.at[rest], summed.at[rest], slow_send.at[1]).wait()
 
 
 def local(nx, ny, constants, pops, label, drive):
     width, height = pops.shape[1], pops.shape[2]
-    count = nx * ny
     send, forward, inverse = constants
     anywhere = pl.BlockSpec(memory_space=pltpu.HBM)
     f32 = jnp.float32
@@ -468,7 +479,7 @@
             pltpu.VMEM((6, height, NZ), f32),
             pltpu.VMEM((width, height, NZ), jnp.int32),
             pltpu.VMEM((3, width, height, NZ), f32),
-            pltpu.VMEM(send.shape, f32),
+            pltpu.VMEM(send.shape[1:], f32),
             pltpu.VMEM(forward.shape, forward.dtype),
             pltpu.VMEM(inverse.shape, inverse.dtype),
             pltpu.VMEM((STEPS, 2, 5, height, NZ), f32),
@@ -477,14 +488,16 @@
             pltpu.VMEM((STEPS + 1, 2, 5 * width, 1, NZ), f32),
             pltpu.VMEM((STEPS, 2, 2, 1, NZ), f32),
             pltpu.VMEM((STEPS + 1, 2, 2, 1, NZ), f32),
-            pltpu.VMEM((count, 2, NZ), f32),
-            pltpu.VMEM((count, 2, NZ), f32),
+            pltpu.VMEM((nx // GROUP, GROUP * ny, 2, NZ), f32),
+            pltpu.VMEM((nx // GROUP, GROUP * ny, 2, NZ), f32),
+            pltpu.VMEM((GROUP * ny, 2, NZ), f32),
+            pltpu.VMEM((GROUP * ny, 2, NZ), f32),
             pltpu.SemaphoreType.DMA((3,)),
             pltpu.SemaphoreType.DMA((3,)),
             pltpu.SemaphoreType.DMA((STEPS, MESSAGES)),
             pltpu.SemaphoreType.DMA((STEPS, MESSAGES)),
-            pltpu.SemaphoreType.DMA,
-            pltpu.SemaphoreType.DMA,
+            pltpu.SemaphoreType.DMA((2,)),
+            pltpu.SemaphoreType.DMA((2,)),
         ],
         compiler_params=pltpu.CompilerParams(
             collective_id=0, has_side_effects=True, vmem_limit_bytes=60 * 1024 * 1024

time: 26.9 us -> 27.8 us (1.033)
  Pallas kernels: 24.9 us -> 25.8 us
    pallas_call x1, Pallas kernels: 24.9 us -> 25.8 us  [local(): pl.pallas_call(functools.partial(kernel, nx, ny), out_shape=(pltpu.VMEM((...]
where the time goes in v6:
time: 27.8 us; the launch traced here: 27.6 us
  Pallas kernels  25.8 us (93%)
  local copies, waits for them, and re-layouts  1.2 us (4%)
  between operations  0.64 us (2%)
    pallas_call x1, Pallas kernels, local(): pl.pallas_call(functools.partial(kernel, nx, ny), out_shape=(pltpu.VMEM((...  25.8 us
    unnamed x2, local copies, waits for them, and re-layouts  1.2 us

profile of v6, /device:TPU:0, one launch (start us, length us, event | category | flops | bytes accessed | tf_op | source)
XLA Modules:
  0.0 27.6 jit_solution(15435849547366409484)
XLA Ops:
  0.6 25.8 %cycle.1 = (f32[3,4,8,128]{3,2,1,0:T(8,128)S(1)}, f32[3,1,2,32]{3,2,1,0:T(2,128)S(1)}) custom-call(f32[19,4,8,128]{3,2,1,0:T(8,128)} %pops_hbm.1, s32[4,8,128]{2,1,0:T(8,128)} %label_hbm.1, f32[3,4,8,128]{3,2,1,0:T(8,128)} %drive_hbm.1, f32[4,8,12,8,128]{4,3,2,1,0:T(8,128)} %constant.6.clone.table_hbm, bf16[2,128,256]{2,1,0:T(8,128)(2,1)} %constant.7.clone.forward_hbm, ...), custom_call_target="tpu_custom_call" | custom-call | tf_op jit(solution)/shard_map/cycle/pallas_call | solution.py:469
  26.4 0.6 %copy.10 = f32[3,4,8,128]{3,2,1,0:T(8,128)} copy(f32[3,4,8,128]{3,2,1,0:T(8,128)S(1)} %get-tuple-element.2) | data formatting | bytes 98304
  27.0 0.6 %copy.11 = f32[3,1,2,32]{3,2,1,0:T(2,128)} copy(f32[3,1,2,32]{3,2,1,0:T(2,128)S(1)} %get-tuple-element.3) | data formatting | bytes 1536

commit v7 on v5

--- a/solution.py
+++ b/solution.py
@@ -38,10 +38,13 @@
 SLOW_VISCOSITY = 0.0004
 PAIRS = [(0, 0), (1, 1), (2, 2), (0, 1), (0, 2), (1, 2)]
 EVEN = 4
-CROSS = {
-    (axis, sign): [i for i in range(19) if VELOCITY[i][axis] == sign] for axis in (0, 1) for sign in (1, -1)
-}
+ORDER = [i for sign in (1, 0, -1) for i in range(19) if VELOCITY[i][0] == sign]
+KEPT = {i: n for n, i in enumerate(ORDER)}
+UP, STAY = 5, 14
+CROSS = {(axis, sign): [i for i in ORDER if VELOCITY[i][axis] == sign] for axis in (0, 1) for sign in (1, -1)}
+PAD = 2
 MESSAGES = 8
+WIDE = 32
 
 
 def wave_table(length):
@@ -160,18 +163,19 @@
 
 def kernel(
     nx, ny, pops_hbm, label_hbm, drive_hbm, table_hbm, forward_hbm, inverse_hbm, momentum, running_ref,
-    state, stress, label, drive, table, forward, inverse_z, face_out, face_in, row_out, row_in, edge_out, edge_in,
-    message, arrived, load_sem, const_sem, halo_send, halo_recv, slow_send, slow_recv,
+    raw, state, stress, label, drive, table, forward, inverse_z, face_out, face_in, row_out, row_in, edge_out, edge_in,
+    message, arrived, load_sem, const_sem, wide_send, wide_recv, halo_send, halo_recv, slow_send, slow_recv,
 ):
-    width = label.shape[0]
+    width = raw.shape[1]
+    own = pl.ds(PAD, width)
     gx = lax.axis_index("gx")
     gy = lax.axis_index("gy")
     count = nx * ny
 
     loads = [
-        pltpu.make_async_copy(pops_hbm, state.at[0], load_sem.at[0]),
-        pltpu.make_async_copy(label_hbm, label, load_sem.at[1]),
-        pltpu.make_async_copy(drive_hbm, drive, load_sem.at[2]),
+        pltpu.make_async_copy(pops_hbm, raw, load_sem.at[0]),
+        pltpu.make_async_copy(label_hbm, label.at[own], load_sem.at[1]),
+        pltpu.make_async_copy(drive_hbm, drive.at[:, own], load_sem.at[2]),
     ]
     constants = [
         pltpu.make_async_copy(table_hbm, table, const_sem.at[0]),
@@ -219,62 +223,123 @@
             device_id_type=MESH,
         )
 
+    def wide():
+        number = iter(range(WIDE))
+
+        def to(ref, src, dst, spot):
+            return pltpu.make_async_remote_copy(
+                src_ref=ref.at[src],
+                dst_ref=ref.at[dst] if ref is not row_out else row_in.at[dst],
+                send_sem=wide_send.at[at := next(number)],
+                recv_sem=wide_recv.at[at],
+                device_id=spot,
+                device_id_type=MESH,
+            )
+
+        every = slice(None)
+        across, along = [], []
+        for sign in (1, -1):
+            spot = (side_x[sign], gy)
+            if sign == 1:
+                parts = [(pl.ds(0, UP), width + PAD, PAD), (pl.ds(0, STAY), width + 1, 1), (pl.ds(0, 19), width, 0)]
+                rows = [(pl.ds(0, 1), width, 0, 3), (pl.ds(1, 3), width, 0, 2), (pl.ds(4, 1), width, 0, 1)]
+                fields = (pl.ds(width, PAD), pl.ds(0, PAD))
+            else:
+                top = width + PAD
+                parts = [
+                    (pl.ds(STAY, UP), 1, top - 1), (pl.ds(UP, STAY), PAD, top), (pl.ds(0, 19), PAD + 1, top + 1)
+                ]
+                rows = [
+                    (pl.ds(4, 1), 1, top - 1, 3), (pl.ds(1, 3), PAD, top, 2), (pl.ds(0, 1), PAD + 1, top + 1, 1)
+                ]
+                fields = (pl.ds(PAD, PAD), pl.ds(top, PAD))
+            for which, here, there in parts:
+                across.append(to(state, (1, which, pl.ds(here, 1)), (1, which, pl.ds(there, 1)), spot))
+            for which, here, there, size in rows:
+                src, dst = pl.ds(here, size), pl.ds(there, size)
+                if ny == 2:
+                    across.append(to(row_out, (1, every, which, src), (1, every, which, dst), (side_x[sign], north)))
+                else:
+                    for turn in (1, -1):
+                        t = slot[turn]
+                        diagonal = (side_x[sign], side_y[turn])
+                        across.append(to(row_out, (1, t, which, src), (1, t, which, dst), diagonal))
+            across.append(to(label, (fields[0],), (fields[1],), spot))
+            across.append(to(drive, (every, fields[0]), (every, fields[1]), spot))
+        for which, first in ((pl.ds(0, 1), PAD + 1), (pl.ds(1, 3), PAD), (pl.ds(4, 1), PAD - 1)):
+            part = pl.ds(first, width)
+            if ny == 2:
+                along.append(to(row_out, (1, every, which, part), (1, every, which, part), (gx, north)))
+            else:
+                for turn in (1, -1):
+                    t = slot[turn]
+                    along.append(to(row_out, (1, t, which, part), (1, t, which, part), (gx, side_y[turn])))
+        return across, along
+
+    def lines_along(step):
+        if ny == 2:
+            return [remote(row_out.at[step + 1], row_in.at[step + 1], step, 2, (gx, north))]
+        return [
+            remote(row_out.at[step + 1, slot[sign]], row_in.at[step + 1, slot[sign]], step, 2 + slot[sign],
+                   (gx, side_y[sign]))
+            for sign in (1, -1)
+        ]
+
     def halo(step):
-        faces, rows = {}, []
+        faces = []
         for sign in (1, -1):
             s = slot[sign]
-            faces[sign] = [remote(face_out.at[step, s], face_in.at[step + 1, s], step, s, (side_x[sign], gy))]
+            faces.append(remote(face_out.at[s], face_in.at[s], step, s, (side_x[sign], gy)))
             if ny == 2:
-                faces[sign].append(
-                    remote(edge_out.at[step, s], edge_in.at[step + 1, s], step, 4 + s, (side_x[sign], north))
-                )
+                faces.append(remote(edge_out.at[s], edge_in.at[s], step, 4 + s, (side_x[sign], north)))
                 continue
             for turn in (1, -1):
                 t = slot[turn]
-                faces[sign].append(
-                    remote(
-                        edge_out.at[step, s, t], edge_in.at[step + 1, s, t], step, 4 + 2 * s + t,
-                        (side_x[sign], side_y[turn]),
-                    )
+                faces.append(
+                    remote(edge_out.at[s, t], edge_in.at[s, t], step, 4 + 2 * s + t, (side_x[sign], side_y[turn]))
                 )
-            rows.append(remote(row_out.at[step, s], row_in.at[step + 1, s], step, 2 + s, (gx, side_y[sign])))
-        if ny == 2:
-            rows.append(remote(row_out.at[step], row_in.at[step + 1], step, 2, (gx, north)))
-        return faces, rows
+        return faces
 
     row_id = lax.broadcasted_iota(jnp.int32, (8, NZ), 0)
 
-    def read(step, fresh, i, p):
+    def read(step, i, p):
         cx, cy, _ = VELOCITY[i]
-        outside = (cx == 1 and p == 0) or (cx == -1 and p == width - 1)
+        if step == 0:
+            return raw[i, p]
+        outside = step == STEPS and ((cx == 1 and p == 0) or (cx == -1 and p == width - 1))
         if outside:
-            value = face_in[step, slot[cx], CROSS[0, cx].index(i)]
+            value = face_in[slot[cx], CROSS[0, cx].index(i)]
         else:
-            value = state[step, i, p]
+            value = state[step, KEPT[i], p + PAD]
         if cy:
             if outside:
-                row = edge_in[step, slot[cx], slot[cy]]
+                row = edge_in[slot[cx], slot[cy]]
             else:
-                row = row_in[step, slot[cy], CROSS[1, cy].index(i) * width + p]
-            value = jnp.where(row_id == fresh[cy], jnp.broadcast_to(row, (8, NZ)), value)
+                row = row_in[step, slot[cy], CROSS[1, cy].index(i), p + PAD]
+            value = jnp.where(row_id == (0 if cy == 1 else 7), jnp.broadcast_to(row, (8, NZ)), value)
         return value
 
     def write(step, i, p, value):
         cx, cy, cz = VELOCITY[i]
+        to = p + cx
+        last = step == STEPS - 1
+        beyond = {0: 1, 1: 1, 2: 0, 3: 0}[step]
+        outside = to < -beyond or to >= width + beyond
+        if outside and not last:
+            return
         if cz:
             value = pltpu.roll(value, cz % NZ, 1)
         if cy:
             value = pltpu.roll(value, cy % 8, 0)
             line = value[0:1] if cy == 1 else value[7:8]
-        outside = (cx == 1 and p == width - 1) or (cx == -1 and p == 0)
         if outside:
-            face_out[step, slot[cx], CROSS[0, cx].index(i)] = value
+            face_out[slot[cx], CROSS[0, cx].index(i)] = value
             if cy:
-                edge_out[step, slot[cx], slot[cy]] = line
+                edge_out[slot[cx], slot[cy]] = line
         else:
-            state[step + 1, i, p + cx] = value
+            state[step + 1, KEPT[i], to + PAD] = value
             if cy:
-                row_out[step, slot[cy], CROSS[1, cy].index(i) * width + p + cx] = line
+                row_out[step + 1, slot[cy], CROSS[1, cy].index(i), to + PAD] = line
 
     def send_copy(far, place):
         return pltpu.make_async_remote_copy(
@@ -291,31 +356,33 @@
         return jnp.where((step == 0) | (step == STEPS - 1), quarter, -quarter)
 
     def measure(step, planes):
-        fresh = {1: jnp.where(step > 0, 0, -1), -1: jnp.where(step > 0, 7, -1)}
         total = [None] * 6
         held = []
         for p in planes:
-            f = [read(step, fresh, i, p) for i in range(19)]
+            f = [read(step, i, p) for i in range(19)]
             rho, j = moments(f)
             inverse = 1.0 / rho
-            thin = jnp.where(label[p] == 2, 0.0, inverse)
+            held.append((p, f, rho, j, inverse))
+            if p < 0 or p >= width:
+                continue
+            thin = jnp.where(label[p + PAD] == 2, 0.0, inverse)
             scaled = [one * thin for one in j]
             for c, (a, b) in enumerate(PAIRS):
                 term = scaled[a] * j[b]
                 total[c] = term if total[c] is None else total[c] + term
-            held.append((p, f, rho, j, inverse))
         for c in range(6):
-            stress[c] += total[c]
+            if total[c] is not None:
+                stress[c] += total[c]
         return held
 
     def finish(step, held):
         phase = phase_of(step)
         for p, f, rho, j, inverse in held:
-            second = label[p] == 1
+            second = label[p + PAD] == 1
             omega = jnp.where(second, 1.1, 1.6)
             strength = jnp.where(second, 0.6 * phase, phase)
-            push = [strength * drive[a, p] for a in range(3)]
-            post = collide(f, rho, j, inverse, 1.0 - omega, omega, push, label[p] == 2)
+            push = [strength * drive[a, p + PAD] for a in range(3)]
+            post = collide(f, rho, j, inverse, 1.0 - omega, omega, push, label[p + PAD] == 2)
             for i in range(19):
                 write(step, i, p, post[i])
 
@@ -323,65 +390,36 @@
         for p in planes:
             finish(step, measure(step, [p]))
 
-    for sign in (1, -1):
-        for k, i in enumerate(CROSS[0, sign]):
-            face_in[0, slot[sign], k] = state[0, i, 0 if sign == 1 else width - 1]
-
-    inner = list(range(1, width - 1))
-    far_side = gx == nx - 1
-
-    def start_step(step):
-        for copy in halo(step - 1)[1]:
-            copy.wait_recv()
-        advance(step, inner)
-
-    def side(step, sign):
-        for copy in halo(step - 1)[0][-sign]:
-            copy.wait_recv()
-        advance(step, [width - 1 if sign == 1 else 0])
-        for copy in halo(step)[0][sign]:
-            copy.start()
-
-    advance(0, [0, width - 1])
+    advance(0, range(width))
     pl.semaphore_wait(barrier, count - 1)
-    faces, rows = halo(0)
-    for copy in faces[1] + faces[-1]:
+    across, along = wide()
+    for copy in across + along:
         copy.start()
-    advance(0, inner)
+    for copy in along:
+        copy.wait_recv()
+    advance(1, range(1, width - 1))
+    for copy in across:
+        copy.wait_recv()
+    advance(1, [0, width - 1, -1, width, -2, width + 1])
+    rows = lines_along(1)
     for copy in rows:
         copy.start()
-
-    def cycle_step(step, carry):
-        start_step(step)
-
-        @pl.when(far_side)
-        def _():
-            side(step, -1)
-            side(step, 1)
-
-        @pl.when(jnp.logical_not(far_side))
-        def _():
-            side(step, 1)
-            side(step, -1)
-
-        for copy in halo(step)[1]:
-            copy.start()
-        return carry
-
-    lax.fori_loop(1, STEPS - 1, cycle_step, 0)
-    step = STEPS - 1
-    start_step(step)
+    for copy in rows:
+        copy.wait_recv()
+    advance(2, range(-1, width + 1))
+    rows = lines_along(2)
+    for copy in rows:
+        copy.start()
     for copy in constants:
         copy.wait()
-    for sign in (1, -1):
-        for copy in halo(step - 1)[0][sign]:
-            copy.wait_recv()
-    held = measure(step, [0, width - 1])
+    for copy in rows:
+        copy.wait_recv()
+    step = STEPS - 1
+    held = measure(step, range(width))
     plain = dot(stress[:EVEN].reshape(8 * EVEN, NZ), forward[0])
     turned = dot(stress[EVEN:].reshape(8 * (6 - EVEN), NZ), forward[1])
     finish(step, held)
-    faces, rows = halo(step)
-    last = faces[1] + faces[-1] + rows
+    last = halo(step) + lines_along(step)
     for copy in last:
         copy.start()
 
@@ -414,7 +452,7 @@
     for copy in last:
         copy.wait_recv()
     for p in range(width):
-        f = [None] + [read(STEPS, {1: 0, -1: 7}, i, p) for i in range(1, 19)]
+        f = [None] + [read(STEPS, i, p) for i in range(1, 19)]
         for axis in range(3):
             value = None
             for i in range(1, 19):
@@ -422,10 +460,8 @@
                 if c:
                     value = c * f[i] if value is None else value + f[i] if c > 0 else value - f[i]
             momentum[axis, p] = value
-    for step in range(STEPS):
-        faces, rows = halo(step)
-        for copy in faces[1] + faces[-1] + rows:
-            copy.wait_send()
+    for copy in across + along + lines_along(1) + lines_along(2) + last:
+        copy.wait_send()
 
     rest = pl.ds(1, count - 1)
     pltpu.make_async_copy(message.at[rest], arrived.at[rest], slow_recv).wait()
@@ -464,23 +500,26 @@
         in_specs=[anywhere] * 6,
         out_specs=(pl.BlockSpec(memory_space=pltpu.VMEM),) * 2,
         scratch_shapes=[
-            pltpu.VMEM((STEPS + 1, 19, width, height, NZ), f32),
+            pltpu.VMEM((19, width, height, NZ), f32),
+            pltpu.VMEM((STEPS + 1, 19, width + 2 * PAD, height, NZ), f32),
             pltpu.VMEM((6, height, NZ), f32),
-            pltpu.VMEM((width, height, NZ), jnp.int32),
-            pltpu.VMEM((3, width, height, NZ), f32),
+            pltpu.VMEM((width + 2 * PAD, height, NZ), jnp.int32),
+            pltpu.VMEM((3, width + 2 * PAD, height, NZ), f32),
             pltpu.VMEM(send.shape, f32),
             pltpu.VMEM(forward.shape, forward.dtype),
             pltpu.VMEM(inverse.shape, inverse.dtype),
-            pltpu.VMEM((STEPS, 2, 5, height, NZ), f32),
-            pltpu.VMEM((STEPS + 1, 2, 5, height, NZ), f32),
-            pltpu.VMEM((STEPS, 2, 5 * width, 1, NZ), f32),
-            pltpu.VMEM((STEPS + 1, 2, 5 * width, 1, NZ), f32),
-            pltpu.VMEM((STEPS, 2, 2, 1, NZ), f32),
-            pltpu.VMEM((STEPS + 1, 2, 2, 1, NZ), f32),
+            pltpu.VMEM((2, 5, height, NZ), f32),
+            pltpu.VMEM((2, 5, height, NZ), f32),
+            pltpu.VMEM((STEPS + 1, 2, 5, width + 2 * PAD, 1, NZ), f32),
+            pltpu.VMEM((STEPS + 1, 2, 5, width + 2 * PAD, 1, NZ), f32),
+            pltpu.VMEM((2, 2, 1, NZ), f32),
+            pltpu.VMEM((2, 2, 1, NZ), f32),
             pltpu.VMEM((count, 2, NZ), f32),
             pltpu.VMEM((count, 2, NZ), f32),
             pltpu.SemaphoreType.DMA((3,)),
             pltpu.SemaphoreType.DMA((3,)),
+            pltpu.SemaphoreType.DMA((WIDE,)),
+            pltpu.SemaphoreType.DMA((WIDE,)),
             pltpu.SemaphoreType.DMA((STEPS, MESSAGES)),
             pltpu.SemaphoreType.DMA((STEPS, MESSAGES)),
             pltpu.SemaphoreType.DMA,

time: 26.9 us -> 26.8 us (level)
  no operation moved by 1% of the time
where the time goes in v7:
time: 26.8 us; the launch traced here: 26.6 us
  Pallas kernels  24.8 us (93%)
  local copies, waits for them, and re-layouts  1.2 us (4%)
  between operations  0.64 us (2%)
    pallas_call x1, Pallas kernels, local(): pl.pallas_call(functools.partial(kernel, nx, ny), out_shape=(pltpu.VMEM((...  24.8 us
    unnamed x2, local copies, waits for them, and re-layouts  1.2 us

profile of v7, /device:TPU:0, one launch (start us, length us, event | category | flops | bytes accessed | tf_op | source)
XLA Modules:
  0.0 26.6 jit_solution(17675257145506920152)
XLA Ops:
  0.6 24.8 %cycle.1 = (f32[3,4,8,128]{3,2,1,0:T(8,128)S(1)}, f32[3,1,2,32]{3,2,1,0:T(2,128)S(1)}) custom-call(f32[19,4,8,128]{3,2,1,0:T(8,128)} %pops_hbm.1, s32[4,8,128]{2,1,0:T(8,128)} %label_hbm.1, f32[3,4,8,128]{3,2,1,0:T(8,128)} %drive_hbm.1, f32[8,12,8,128]{3,2,1,0:T(8,128)} %constant.6.clone.table_hbm, bf16[2,128,256]{2,1,0:T(8,128)(2,1)} %constant.7.clone.forward_hbm, ...), custom_call_target="tpu_custom_call" | custom-call | tf_op jit(solution)/shard_map/cycle/pallas_call | solution.py:494
  25.4 0.6 %copy.10 = f32[3,4,8,128]{3,2,1,0:T(8,128)} copy(f32[3,4,8,128]{3,2,1,0:T(8,128)S(1)} %get-tuple-element.2) | data formatting | bytes 98304
  26.1 0.6 %copy.11 = f32[3,1,2,32]{3,2,1,0:T(2,128)} copy(f32[3,1,2,32]{3,2,1,0:T(2,128)S(1)} %get-tuple-element.3) | data formatting | bytes 1536

commit v8 on v7

--- a/solution.py
+++ b/solution.py
@@ -237,7 +237,7 @@
             )
 
         every = slice(None)
-        across, along = [], []
+        stages, along = ([], [], []), []
         for sign in (1, -1):
             spot = (side_x[sign], gy)
             if sign == 1:
@@ -253,19 +253,19 @@
                     (pl.ds(4, 1), 1, top - 1, 3), (pl.ds(1, 3), PAD, top, 2), (pl.ds(0, 1), PAD + 1, top + 1, 1)
                 ]
                 fields = (pl.ds(PAD, PAD), pl.ds(top, PAD))
-            for which, here, there in parts:
-                across.append(to(state, (1, which, pl.ds(here, 1)), (1, which, pl.ds(there, 1)), spot))
-            for which, here, there, size in rows:
+            for stage, (which, here, there) in zip(stages, parts):
+                stage.append(to(state, (1, which, pl.ds(here, 1)), (1, which, pl.ds(there, 1)), spot))
+            for stage, (which, here, there, size) in zip(stages, rows):
                 src, dst = pl.ds(here, size), pl.ds(there, size)
                 if ny == 2:
-                    across.append(to(row_out, (1, every, which, src), (1, every, which, dst), (side_x[sign], north)))
+                    stage.append(to(row_out, (1, every, which, src), (1, every, which, dst), (side_x[sign], north)))
                 else:
                     for turn in (1, -1):
                         t = slot[turn]
                         diagonal = (side_x[sign], side_y[turn])
-                        across.append(to(row_out, (1, t, which, src), (1, t, which, dst), diagonal))
-            across.append(to(label, (fields[0],), (fields[1],), spot))
-            across.append(to(drive, (every, fields[0]), (every, fields[1]), spot))
+                        stage.append(to(row_out, (1, t, which, src), (1, t, which, dst), diagonal))
+            stages[1].append(to(label, (fields[0],), (fields[1],), spot))
+            stages[1].append(to(drive, (every, fields[0]), (every, fields[1]), spot))
         for which, first in ((pl.ds(0, 1), PAD + 1), (pl.ds(1, 3), PAD), (pl.ds(4, 1), PAD - 1)):
             part = pl.ds(first, width)
             if ny == 2:
@@ -274,16 +274,20 @@
                 for turn in (1, -1):
                     t = slot[turn]
                     along.append(to(row_out, (1, t, which, part), (1, t, which, part), (gx, side_y[turn])))
-        return across, along
+        return stages, along
 
     def lines_along(step):
+        beyond = 1 if step == 1 else 0
+        part = pl.ds(PAD - beyond, width + 2 * beyond)
+        every = slice(None)
         if ny == 2:
-            return [remote(row_out.at[step + 1], row_in.at[step + 1], step, 2, (gx, north))]
-        return [
-            remote(row_out.at[step + 1, slot[sign]], row_in.at[step + 1, slot[sign]], step, 2 + slot[sign],
-                   (gx, side_y[sign]))
-            for sign in (1, -1)
-        ]
+            where = (step + 1, every, every, part)
+            return [remote(row_out.at[where], row_in.at[where], step, 2, (gx, north))]
+        copies = []
+        for sign in (1, -1):
+            where = (step + 1, slot[sign], every, part)
+            copies.append(remote(row_out.at[where], row_in.at[where], step, 2 + slot[sign], (gx, side_y[sign])))
+        return copies
 
     def halo(step):
         faces = []
@@ -392,15 +396,16 @@
 
     advance(0, range(width))
     pl.semaphore_wait(barrier, count - 1)
-    across, along = wide()
-    for copy in across + along:
+    stages, along = wide()
+    for copy in stages[0] + along + stages[1] + stages[2]:
         copy.start()
     for copy in along:
         copy.wait_recv()
     advance(1, range(1, width - 1))
-    for copy in across:
-        copy.wait_recv()
-    advance(1, [0, width - 1, -1, width, -2, width + 1])
+    for distance, stage in enumerate(stages):
+        for copy in stage:
+            copy.wait_recv()
+        advance(1, [-distance, width - 1 + distance])
     rows = lines_along(1)
     for copy in rows:
         copy.start()
@@ -460,7 +465,7 @@
                 if c:
                     value = c * f[i] if value is None else value + f[i] if c > 0 else value - f[i]
             momentum[axis, p] = value
-    for copy in across + along + lines_along(1) + lines_along(2) + last:
+    for copy in stages[0] + stages[1] + stages[2] + along + lines_along(1) + lines_along(2) + last:
         copy.wait_send()
 
     rest = pl.ds(1, count - 1)

time: 26.8 us -> 25.9 us (0.966)
  Pallas kernels: 24.8 us -> 23.9 us
    pallas_call x1, Pallas kernels: 24.8 us -> 23.9 us  [local(): pl.pallas_call(functools.partial(kernel, nx, ny), out_shape=(pltpu.VMEM((...]
where the time goes in v8:
time: 25.9 us; the launch traced here: 25.7 us
  Pallas kernels  23.9 us (92%)
  local copies, waits for them, and re-layouts  1.2 us (5%)
  between operations  0.64 us (2%)
    pallas_call x1, Pallas kernels, local(): pl.pallas_call(functools.partial(kernel, nx, ny), out_shape=(pltpu.VMEM((...  23.9 us
    unnamed x2, local copies, waits for them, and re-layouts  1.2 us

profile of v8, /device:TPU:0, one launch (start us, length us, event | category | flops | bytes accessed | tf_op | source)
XLA Modules:
  0.0 25.7 jit_solution(6818722044119794776)
XLA Ops:
  0.6 23.9 %cycle.1 = (f32[3,4,8,128]{3,2,1,0:T(8,128)S(1)}, f32[3,1,2,32]{3,2,1,0:T(2,128)S(1)}) custom-call(f32[19,4,8,128]{3,2,1,0:T(8,128)} %pops_hbm.1, s32[4,8,128]{2,1,0:T(8,128)} %label_hbm.1, f32[3,4,8,128]{3,2,1,0:T(8,128)} %drive_hbm.1, f32[8,12,8,128]{3,2,1,0:T(8,128)} %constant.6.clone.table_hbm, bf16[2,128,256]{2,1,0:T(8,128)(2,1)} %constant.7.clone.forward_hbm, ...), custom_call_target="tpu_custom_call" | custom-call | tf_op jit(solution)/shard_map/cycle/pallas_call | solution.py:499
  24.5 0.6 %copy.10 = f32[3,4,8,128]{3,2,1,0:T(8,128)} copy(f32[3,4,8,128]{3,2,1,0:T(8,128)S(1)} %get-tuple-element.2) | data formatting | bytes 98304
  25.1 0.6 %copy.11 = f32[3,1,2,32]{3,2,1,0:T(2,128)} copy(f32[3,1,2,32]{3,2,1,0:T(2,128)S(1)} %get-tuple-element.3) | data formatting | bytes 1536

commit v9 on v8

--- a/solution.py
+++ b/solution.py
@@ -425,9 +425,6 @@
     turned = dot(stress[EVEN:].reshape(8 * (6 - EVEN), NZ), forward[1])
     finish(step, held)
     last = halo(step) + lines_along(step)
-    for copy in last:
-        copy.start()
-
     lines = []
     for c in range(6):
         tile = plain[8 * c : 8 * c + 8] if c < EVEN else turned[8 * (c - EVEN) : 8 * (c - EVEN) + 8]
@@ -453,6 +450,8 @@
 
         lax.fori_loop(0, count // 4, each, 0)
     over_others(lambda far, place: send_copy(far, place).start())
+    for copy in last:
+        copy.start()
 
     for copy in last:
         copy.wait_recv()

time: 25.9 us -> 25.9 us (level)
  no operation moved by 1% of the time
where the time goes in v9:
time: 25.9 us; the launch traced here: 25.8 us
  Pallas kernels  23.9 us (92%)
  local copies, waits for them, and re-layouts  1.2 us (5%)
  between operations  0.64 us (2%)
    pallas_call x1, Pallas kernels, local(): pl.pallas_call(functools.partial(kernel, nx, ny), out_shape=(pltpu.VMEM((...  23.9 us
    unnamed x2, local copies, waits for them, and re-layouts  1.2 us

profile of v9, /device:TPU:0, one launch (start us, length us, event | category | flops | bytes accessed | tf_op | source)
XLA Modules:
  0.0 25.8 jit_solution(4228517554738744041)
XLA Ops:
  0.6 23.9 %cycle.1 = (f32[3,4,8,128]{3,2,1,0:T(8,128)S(1)}, f32[3,1,2,32]{3,2,1,0:T(2,128)S(1)}) custom-call(f32[19,4,8,128]{3,2,1,0:T(8,128)} %pops_hbm.1, s32[4,8,128]{2,1,0:T(8,128)} %label_hbm.1, f32[3,4,8,128]{3,2,1,0:T(8,128)} %drive_hbm.1, f32[8,12,8,128]{3,2,1,0:T(8,128)} %constant.6.clone.table_hbm, bf16[2,128,256]{2,1,0:T(8,128)(2,1)} %constant.7.clone.forward_hbm, ...), custom_call_target="tpu_custom_call" | custom-call | tf_op jit(solution)/shard_map/cycle/pallas_call | solution.py:498
  24.6 0.6 %copy.10 = f32[3,4,8,128]{3,2,1,0:T(8,128)} copy(f32[3,4,8,128]{3,2,1,0:T(8,128)S(1)} %get-tuple-element.2) | data formatting | bytes 98304
  25.2 0.6 %copy.11 = f32[3,1,2,32]{3,2,1,0:T(2,128)} copy(f32[3,1,2,32]{3,2,1,0:T(2,128)S(1)} %get-tuple-element.3) | data formatting | bytes 1536
